TPU v7x, 128 devices: a whole 4x4x4 slice. The times are simulated.
128 devices in a mesh: lat: 32 (over y, x_lo, z), lon: 2 (over core), ens: 2 (over x_hi).
Axes of the slice: x: 4 (x_hi: 2, x_lo: 2; x = x_hi * 2 + x_lo), y: 4, z: 4, core: 2. Of those that a mesh axis runs over, the one named last changes fastest.
Arguments:
- fields: bfloat16 [2, 64, 1440, 256], P('ens', 'lat', 'lon'), may hold values from -6 to 6
- cotangent: bfloat16 [2, 64, 1440, 256], P('ens', 'lat', 'lon'), may hold values from -6 to 6
- weights: bfloat16 [9, 256, 32], replicated, may hold values from -0.375 to 0.375
- basis_values: bfloat16 [64, 5, 9, 5], replicated, may hold values from 0 to 0.5
- support: int32 [64, 5], replicated, may hold values from -2 to 65, as said below
- counts: int32 [64], replicated, may hold values from 1 to 5, as said below
Outputs:
- mixed_output: bfloat16 [2, 64, 1440, 256], P('ens', 'lat', 'lon')
- input_grad: bfloat16 [2, 64, 1440, 256], P('ens', 'lat', 'lon')
- weight_grad: float32 [9, 256, 32], P(None, 'lat')
Inputs may be any that keep to these rules, and one draw needn't show every extreme that they name: `support`: the first counts[i] entries of row i are consecutive increasing virtual rows, each within 2 of i; later entries equal i. Row 0 holds -2 and row 63 holds 65. `counts`: rows 0 and 63 use all slots.
All inputs are finite; a program needn't handle non-finite values.
Results may differ from a plain program's by a relative error of at most 0.005.
Values may be sent and summed in bfloat16 or wider, within the bound.
A program may use at most 256 MiB of HBM per device.

v0:
```python
import math

import jax
import jax.numpy as jnp
from jax import lax
from jax.sharding import PartitionSpec as P

C = 256
GW = 32
K = 9
HDEPTH = 2
HW = 2
SMAX = 5
WIN = 5


def with_halo(cells, sides, width):
    for axis, dim in sides:
        count = lax.axis_size(axis)
        ends = count - 1
        head = lax.slice_in_dim(cells, 0, width, axis=dim)
        tail = lax.slice_in_dim(cells, cells.shape[dim] - width, cells.shape[dim], axis=dim)
        cells = jnp.concatenate(
            [
                lax.ppermute(tail, axis, [(i, (i + 1) % count) for i in range(ends)]),
                cells,
                lax.ppermute(head, axis, [((i + 1) % count, i) for i in range(ends)]),
            ],
            axis=dim,
        )
    return cells


def kernel_rows(basis_rows, count_rows, weights):
    slot_ids = jnp.arange(basis_rows.shape[1], dtype=jnp.int32)
    alive_mask = (slot_ids[None, :] < count_rows[:, None]).astype(jnp.float32)
    masked = basis_rows.astype(jnp.float32) * alive_mask[:, :, None, None]
    mixing = weights.astype(jnp.float32).reshape(
        weights.shape[0], weights.shape[1] // weights.shape[2], weights.shape[2], weights.shape[2]
    )
    combined = jnp.einsum("uskm,kgoc->usmgco", masked, mixing, precision=lax.Precision.HIGHEST)
    return (masked, combined.astype(jnp.bfloat16))


def dense_blocks(combined, lane_width):
    rows_here, slots, offsets, groups, width_in, width_out = combined.shape
    per_block = lane_width // width_in
    block_count = groups // per_block
    grouped = combined.astype(jnp.float32).reshape(
        rows_here, slots, offsets, block_count, per_block, width_in, width_out
    )
    identity = jnp.eye(per_block, dtype=jnp.float32)
    spread = grouped[:, :, :, :, :, :, None, :] * identity[:, None, :, None]
    spread = spread.reshape(rows_here, slots, offsets, block_count, lane_width, lane_width)
    forward_kernel = jnp.transpose(spread, (0, 3, 1, 2, 4, 5)).reshape(
        rows_here, block_count, slots * offsets * lane_width, lane_width
    )
    adjoint_kernel = jnp.transpose(spread, (0, 3, 2, 5, 1, 4)).reshape(
        rows_here, block_count, offsets * lane_width, slots * lane_width
    )
    return (forward_kernel.astype(jnp.bfloat16), adjoint_kernel.astype(jnp.bfloat16))


def shards(fields, cotangent, weights, basis_values, support, counts):
    lat_index = lax.axis_index("lat")
    lat_count = lax.axis_size("lat")
    lon_index = lax.axis_index("lon")
    lon_count = lax.axis_size("lon")
    ens_count = lax.axis_size("ens")
    band_rows = fields.shape[1]
    sector_cols = fields.shape[2]
    lat_total = basis_values.shape[0]
    lane_width = min(C, 128)
    block_count = C // lane_width
    per_block = lane_width // GW
    panel_count = band_rows + 2 * HDEPTH
    top_pole = lat_index == 0
    bottom_pole = lat_index == lat_count - 1
    stacked = jnp.stack([fields[0], cotangent[0]], axis=0)
    rimmed = with_halo(stacked, (("lat", 1),), HDEPTH)
    whole_band = lax.all_gather(rimmed, "lon", axis=2, tiled=True)
    half_turn = whole_band.shape[2] // 2
    north_far = jnp.roll(jnp.flip(whole_band[:, HDEPTH : 2 * HDEPTH], 1), half_turn, axis=2)
    south_far = jnp.roll(
        jnp.flip(whole_band[:, band_rows : band_rows + HDEPTH], 1), half_turn, axis=2
    )
    whole_band = jnp.concatenate(
        [
            jnp.where(top_pole, north_far, whole_band[:, :HDEPTH]),
            whole_band[:, HDEPTH : band_rows + HDEPTH],
            jnp.where(bottom_pole, south_far, whole_band[:, band_rows + HDEPTH :]),
        ],
        axis=1,
    )
    wrapped = jnp.concatenate(
        [whole_band[:, :, whole_band.shape[2] - HW :], whole_band, whole_band[:, :, :HW]], axis=2
    )
    padded_panel = lax.dynamic_slice_in_dim(
        wrapped, lon_index * sector_cols, sector_cols + 2 * HW, 2
    )
    source = padded_panel[0]
    grads_panel = padded_panel[1]
    base_row = lat_index * band_rows - HDEPTH
    virtual = base_row + jnp.arange(panel_count, dtype=jnp.int32)
    real_rows = jnp.where(
        virtual < 0,
        -1 - virtual,
        jnp.where(virtual >= lat_total, 2 * lat_total - 1 - virtual, virtual),
    )
    row_basis = jnp.take(basis_values, real_rows, axis=0)
    row_counts = jnp.take(counts, real_rows, axis=0)
    row_support = jnp.take(support, real_rows, axis=0)
    masked, combined = kernel_rows(row_basis, row_counts, weights)
    forward_kernel, adjoint_kernel = dense_blocks(combined, lane_width)
    identity = jnp.eye(per_block, dtype=jnp.float32)

    def forward_row(local_row):
        panel_row = local_row + HDEPTH
        picked_rows = jnp.take(source, row_support[panel_row] - base_row, axis=0)
        grad_out = cotangent[0, local_row]
        out_blocks = []
        grad_blocks = []
        for block in range(block_count):
            low = block * lane_width
            window = jnp.concatenate(
                [
                    picked_rows[
                        slot, shift_index : shift_index + sector_cols, low : low + lane_width
                    ]
                    for slot in range(SMAX)
                    for shift_index in range(WIN)
                ],
                axis=1,
            )
            out_blocks.append(
                jnp.dot(
                    window, forward_kernel[panel_row, block], preferred_element_type=jnp.float32
                )
            )
            block_grad = lax.dot_general(
                window,
                grad_out[:, low : low + lane_width],
                (((0,), (0,)), ((), ())),
                preferred_element_type=jnp.float32,
            )
            block_grad = block_grad.reshape(SMAX, WIN, per_block, GW, per_block, GW)
            grad_blocks.append(
                jnp.einsum(
                    "smpcqo,pq->smpco", block_grad, identity, precision=lax.Precision.HIGHEST
                )
            )
        kernel_grad = jnp.concatenate(grad_blocks, axis=2)
        weight_part = jnp.einsum(
            "skm,smgco->kgoc", masked[panel_row], kernel_grad, precision=lax.Precision.HIGHEST
        )
        out_row = jnp.concatenate(out_blocks, axis=1).astype(jnp.bfloat16)
        return (out_row, weight_part)

    out_rows, weight_parts = lax.map(forward_row, jnp.arange(band_rows, dtype=jnp.int32))
    low_row = lat_index * band_rows

    def adjoint_row(panel_row, buffer):
        grad_rows = grads_panel[panel_row]
        block_terms = []
        for block in range(block_count):
            low = block * lane_width
            window = jnp.concatenate(
                [
                    grad_rows[
                        2 * HW - shift_index : 2 * HW - shift_index + sector_cols,
                        low : low + lane_width,
                    ]
                    for shift_index in range(WIN)
                ],
                axis=1,
            )
            block_terms.append(
                jnp.dot(
                    window, adjoint_kernel[panel_row, block], preferred_element_type=jnp.float32
                )
            )
        row_virtual = virtual[panel_row]
        targets = row_support[panel_row]
        targets = jnp.where(
            row_virtual < 0,
            -1 - targets,
            jnp.where(row_virtual >= lat_total, 2 * lat_total - 1 - targets, targets),
        )
        target_spots = targets - low_row
        target_spots = jnp.where(
            (target_spots >= 0) & (target_spots < band_rows), target_spots, band_rows
        )
        for slot in range(SMAX):
            piece = jnp.concatenate(
                [term[:, slot * lane_width : (slot + 1) * lane_width] for term in block_terms],
                axis=1,
            )
            buffer = buffer.at[target_spots[slot]].add(piece)
        return buffer

    buffer = lax.fori_loop(
        0, panel_count, adjoint_row, jnp.zeros((band_rows + 1, sector_cols, C), jnp.float32)
    )
    input_grad = buffer[:band_rows].astype(jnp.bfloat16)[None]
    grad_scale = 1.0 / math.sqrt(lat_total * sector_cols * lon_count * ens_count * fields.shape[0])
    weight_local = (jnp.sum(weight_parts, axis=0) * grad_scale).reshape(K, C, GW)
    share_width = C // lat_count
    summed_all = lax.psum(weight_local, ("lat", "lon", "ens"))
    weight_grad = lax.dynamic_slice_in_dim(summed_all, lat_index * share_width, share_width, 1)
    return (out_rows[None], input_grad, weight_grad)


def solution(mesh):
    placed = (P("ens", "lat", "lon", None), P("ens", "lat", "lon", None), P(), P(), P(), P())
    return jax.shard_map(
        shards,
        mesh=mesh,
        in_specs=placed,
        out_specs=(
            P("ens", "lat", "lon", None),
            P("ens", "lat", "lon", None),
            P(None, "lat", None),
        ),
        check_vma=False,
    )
```

profile of v0, /device:TPU:1, one launch (start us, length us, event | category | flops | bytes accessed | tf_op | source)
XLA Modules:
  0.0 823.6 jit_solution(5319367816090854085)
XLA Ops:
  9.6 4.6 collective-permute-start
  15.5 29.5 %collective-permute-done = bf16[2,2,720,256]{3,2,1,0:T(8,128)(2,1)S(1)} collective-permute-done((bf16[2,2,720,256]{3,2,1,0:T(8,128)(2,1)S(1)}, bf16[2,2,720,256]{3,2,1,0:T(8,128)(2,1)S(1)}, u32[]{:S(2)}, u32[]{:S(2)}) %collective-permute-start) | collective-permute-done | bytes 1474592 | tf_op jit(solution)/shard_map/ppermute | solution.py:25
  45.0 4.1 collective-permute-done.1
  55.0 23.2 %convert_convert_fusion = f32[6,5,5,8,32,32]{5,0,4,3,2,1:T(8,128)} fusion(bf16[9,8,32,32,1,1]{3,0,2,1,5,4:T(8,128)(2,1)S(1)} %bitcast.465, f32[6,5,9,5,1,1]{2,3,1,0,5,4:T(8,128)S(1)} %get-tuple-element.629), kind=kOutput, calls=%fused_computation.203 | convolution fusion | flops 135168000 | bytes 5068056 | tf_op jit(solution)/shard_map/uskm,kgoc->usmgco/dot_general | solution.py:41
  78.2 24.5 %copy.58 = f32[6,5,5,2,4,32,32]{6,5,4,3,2,1,0:T(8,128)} copy(f32[6,5,5,2,4,32,32]{5,0,6,4,3,2,1:T(8,128)} %bitcast.462) | data formatting | bytes 9830400 | tf_op jit(solution)/shard_map/mul | solution.py:53
  102.7 31.5 %mul.59 = f32[6,5,5,2,4,32,4,32]{7,6,5,4,3,2,1,0:T(4,128)} broadcast(f32[6,5,5,2,4,32,32]{6,5,4,3,2,1,0:T(8,128)} %copy.58), dimensions={0,1,2,3,4,5,7} | broadcast | bytes 24576000 | tf_op jit(solution)/shard_map/mul | solution.py:53
  134.2 58.5 %mul.60 = f32[6,5,5,2,128,128]{5,4,3,2,1,0:T(8,128)} reshape(f32[6,5,5,2,4,32,4,32]{7,6,5,4,3,2,1,0:T(4,128)} %mul.59) | data formatting | bytes 39321600 | tf_op jit(solution)/shard_map/mul | solution.py:53
  192.9 17.0 %fusion.95 = (bf16[6,2,5,128,5,128]{3,5,1,2,4,0:T(8,128)(2,1)}, bf16[6,2,5,5,128,128]{5,4,1,3,2,0:T(8,128)(2,1)}) fusion(f32[6,5,5,2,128,128]{5,4,3,2,1,0:T(8,128)} %mul.60, f32[128,128]{1,0:T(8,128)S(1)} %mul.62), kind=kLoop, calls=%fused_computation.206 | loop fusion | flops 9830400 | bytes 39387136 | tf_op jit(solution)/shard_map/convert_element_type | solution.py:61
  209.9 18.5 %copy.61 = bf16[6,2,5,128,5,128]{5,4,3,2,1,0:T(8,128)(2,1)} copy(bf16[6,2,5,128,5,128]{3,5,1,2,4,0:T(8,128)(2,1)} %get-tuple-element.617) | data formatting | bytes 19660800 | tf_op jit(solution)/shard_map/convert_element_type | solution.py:61
  228.4 22.6 %convert_element_type.68 = bf16[6,2,640,640]{3,2,1,0:T(8,128)(2,1)} reshape(bf16[6,2,5,128,5,128]{5,4,3,2,1,0:T(8,128)(2,1)} %copy.61) | data formatting | bytes 19660800 | tf_op jit(solution)/shard_map/convert_element_type | solution.py:61
  251.7 12.0 %copy.59 = bf16[6,2,5,5,128,128]{5,4,3,2,1,0:T(8,128)(2,1)} copy(bf16[6,2,5,5,128,128]{5,4,1,3,2,0:T(8,128)(2,1)} %get-tuple-element.618) | data formatting | bytes 19660800 | tf_op jit(solution)/shard_map/convert_element_type | solution.py:61
  270.8 5.0 slice_select_fusion.1
  280.4 42.8 %concatenate.142 = bf16[2,6,1444,256]{3,2,1,0:T(8,128)(2,1)} concatenate(bf16[2,6,2,256]{3,2,1,0:T(2,128)(2,1)S(1)} %get-tuple-element.624, bf16[2,6,1440,256]{3,2,1,0:T(8,128)(2,1)} %copy-done.6, bf16[2,6,2,256]{3,2,1,0:T(2,128)(2,1)S(1)} %get-tuple-element.623), dimensions={2} | concatenate | bytes 17743872 | tf_op jit(solution)/shard_map/concatenate | solution.py:95
  323.2 5.5 dynamic-slice_bitcast_fusion.2
  328.9 172.1 %while.34 = (s32[]{:T(128)}, f32[3,720,256]{2,1,0:T(8,128)S(1)}, s32[6]{0:T(128)S(1)}, s32[6,5]{1,0:T(8,128)S(1)}, s32[]{:T(128)}, /*index=5*/bf16[6,724,256]{2,...) while((s32[]{:T(128)}, f32[3,720,256]{2,1,0:T(8,128)S(1)}, ...), condition=%wide.region_8.9_spmd, body=%wide.region_2.8_spmd.sunk | while | flops 1182412928 | bytes 31503876 | solution.py:201
  501.0 159.2 %while.35 = (s32[]{:T(128)}, bf16[2,720,256]{2,1,0:T(8,128)(2,1)}, f32[2,9,8,32,32]{3,1,4,2,0:T(8,128)}, s32[2]{0:T(128)S(1)}, s32[6,5]{1,0:T(8,128)S(1)}, /*ind...) while((s32[]{:T(128)}, bf16[2,720,256]{2,1,0:T(8,128)(2,1)}, ...), condition=%wide.region_1.2_spmd.clone.clone, body=%wide.region_0.1_spmd.clone.clone.sunk | while | flops 2393298944 | bytes 161651328 | solution.py:159
  503.1 3.6 gather_fusion
  518.5 5.0 fusion.231
  523.5 6.1 reshape.527
  529.7 14.5 %fusion.232 = f32[4,1,5,5,32,32]{5,1,4,3,2,0:T(1,128)} fusion(f32[4,4,1,1,1,1]{1,2,5,4,3,0:T(1,128)S(1)} %bitcast.466, f32[5,5,4,32,4,32]{5,4,3,2,1,0:T(4,128)} %reshape.527), kind=kOutput, calls=%fused_computation.61.clone.1 | convolution fusion | flops 4915200 | bytes 2048064 | tf_op jit(solution)/shard_map/while/body/eval_jaxpr/smpcqo,pq->smpco/dot_general | solution.py:148
  547.0 6.1 reshape.528
  553.0 13.7 %fusion.234 = f32[4,1,5,5,32,32]{5,1,4,3,2,0:T(1,128)S(1)} fusion(f32[4,4,1,1,1,1]{1,2,5,4,3,0:T(1,128)S(1)} %bitcast.467, f32[5,5,4,32,4,32]{5,4,3,2,1,0:T(4,128)} %reshape.528), kind=kOutput, calls=%fused_computation.63.clone.1 | convolution fusion | flops 4915200 | bytes 2048064 | tf_op jit(solution)/shard_map/while/body/eval_jaxpr/smpcqo,pq->smpco/dot_general | solution.py:148
  569.4 4.4 bitcast_dynamic-update-slice_fusion.2
  582.7 3.6 gather_fusion
  598.0 5.0 fusion.231
  603.0 6.1 reshape.527
  609.2 14.5 %fusion.232 = f32[4,1,5,5,32,32]{5,1,4,3,2,0:T(1,128)} fusion(f32[4,4,1,1,1,1]{1,2,5,4,3,0:T(1,128)S(1)} %bitcast.466, f32[5,5,4,32,4,32]{5,4,3,2,1,0:T(4,128)} %reshape.527), kind=kOutput, calls=%fused_computation.61.clone.1 | convolution fusion | flops 4915200 | bytes 2048064 | tf_op jit(solution)/shard_map/while/body/eval_jaxpr/smpcqo,pq->smpco/dot_general | solution.py:148
  626.5 6.1 reshape.528
  632.5 13.7 %fusion.234 = f32[4,1,5,5,32,32]{5,1,4,3,2,0:T(1,128)S(1)} fusion(f32[4,4,1,1,1,1]{1,2,5,4,3,0:T(1,128)S(1)} %bitcast.467, f32[5,5,4,32,4,32]{5,4,3,2,1,0:T(4,128)} %reshape.528), kind=kOutput, calls=%fused_computation.63.clone.1 | convolution fusion | flops 4915200 | bytes 2048064 | tf_op jit(solution)/shard_map/while/body/eval_jaxpr/smpcqo,pq->smpco/dot_general | solution.py:148
  648.9 4.4 bitcast_dynamic-update-slice_fusion.2
  660.2 4.2 reduce_sum.9
  670.9 143.7 %all-reduce.2.cloned.1.call-done = f32[9,256,32]{1,2,0:T(8,128)} async-done(((f32[9,256,32]{1,2,0:T(8,128)}), f32[9,256,32]{1,2,0:T(8,128)}) %all-reduce.2.cloned.1.call-update) | async-done | bytes 294928 | tf_op jit(solution)/shard_map/psum | solution.py:208
  (314 shorter events, 182.4 us)
Async XLA Ops:
  7.2 44.8 %copy-start = (s32[64]{0:T(128)S(1)}, s32[64]{0:T(128)}, u32[]{:S(2)}) copy-start(s32[64]{0:T(128)} %param.25) | copy-start | bytes 772
  7.2 256.6 %all-gather.2.cloned.1.call-start = ((), (), s32[]{:S(2)}) async-start(), calls=%async_computation | async-start | bytes 13271040 | tf_op jit(solution)/shard_map/all_gather | solution.py:81
  9.6 41.9 %copy-start.10 = (bf16[64,5,9,5]{0,3,2,1:T(8,128)(2,1)S(1)}, bf16[64,5,9,5]{0,3,2,1:T(8,128)(2,1)}, u32[]{:S(2)}) copy-start(bf16[64,5,9,5]{0,3,2,1:T(8,128)(2,1)} %param.23) | copy-start | bytes 86404
  9.6 35.4 %collective-permute-start = (bf16[2,2,720,256]{3,2,1,0:T(8,128)(2,1)S(1)}, bf16[2,2,720,256]{3,2,1,0:T(8,128)(2,1)S(1)}, u32[]{:S(2)}, u32[]{:S(2)}) collective-permute-start(bf16[2,2,720,256]{3,2,1,0:T(8,128)(2,1)S(1)} %constant_dynamic-update-slice_fusion), channel_id=1, source_target_pairs={{0,4},{4,8},{8,12},{12,16},{16,20},{20,24},{24,28},{28,32},{32,36}... | collective-permute-start | bytes 4423688 | tf_op jit(solution)/shard_map/ppermute | solution.py:25
  14.2 34.9 %collective-permute-start.1 = (bf16[2,2,720,256]{3,2,1,0:T(8,128)(2,1)S(1)}, bf16[2,2,720,256]{3,2,1,0:T(8,128)(2,1)S(1)}, u32[]{:S(2)}, u32[]{:S(2)}) collective-permute-start(bf16[2,2,720,256]{3,2,1,0:T(8,128)(2,1)S(1)} %constant_dynamic-update-slice_fusion), channel_id=1, source_target_pairs={{4,0},{8,4},{12,8},{16,12},{20,16},{24,20},{28,24},{32,28},{36,32}... | collective-permute-start | bytes 4423688 | tf_op jit(solution)/shard_map/ppermute | solution.py:27
  51.4 763.2 %all-reduce.2.cloned.1.call-start = ((), (), s32[]{:S(2)}) async-start(), calls=%async_computation.1 | async-start | bytes 589824 | tf_op jit(solution)/shard_map/psum | solution.py:208
  228.4 22.6 %copy-start.12 = (s32[64,5]{0,1:T(8,128)S(1)}, s32[64,5]{0,1:T(8,128)}, u32[]{:S(2)}) copy-start(s32[64,5]{0,1:T(8,128)} %param.24) | copy-start | bytes 3844
  323.2 5.7 copy-start.11
  380.4 4.6 copy-start.5
  409.0 4.6 copy-start.5
  494.8 4.6 copy-start.5
  523.5 20.7 %slice-start = ((s8[4608000]{0:T(1024)(128)(4,1)}), s8[413696]{0:T(1024)(128)(4,1)S(1)}, s32[]{:S(2)}) async-start(s8[4608000]{0:T(1024)(128)(4,1)} %bitcast.456), calls=%async_computation.2 | async-start | bytes 827392 | tf_op jit(solution)/shard_map/while
  529.7 14.5 %slice-start.1 = ((s8[4608000]{0:T(1024)(128)(4,1)}), s8[4194304]{0:T(1024)(128)(4,1)S(1)}, s32[]{:S(2)}) async-start(s8[4608000]{0:T(1024)(128)(4,1)} %bitcast.456), calls=%async_computation.3 | async-start | bytes 8388608 | tf_op jit(solution)/shard_map/while
  553.0 13.7 %copy-start.2 = (f32[4,1,5,5,32,32]{5,1,4,3,2,0:T(1,128)S(1)}, f32[4,1,5,5,32,32]{5,1,4,3,2,0:T(1,128)}, u32[]{:S(2)}) copy-start(f32[4,1,5,5,32,32]{5,1,4,3,2,0:T(1,128)} %fusion.232) | copy-start | bytes 1228804 | tf_op jit(solution)/shard_map/while
  553.0 16.4 %copy-start.7 = (f32[2,9,8,32,32]{3,1,4,2,0:T(8,128)S(1)}, f32[2,9,8,32,32]{3,1,4,2,0:T(8,128)}, u32[]{:S(2)}) copy-start(f32[2,9,8,32,32]{3,1,4,2,0:T(8,128)} %get-tuple-element.914) | copy-start | bytes 1769476 | tf_op jit(solution)/shard_map/while
  553.0 20.9 %slice-start.2 = ((s8[4608000]{0:T(1024)(128)(4,1)}), s8[4194304]{0:T(1024)(128)(4,1)S(1)}, s32[]{:S(2)}) async-start(s8[4608000]{0:T(1024)(128)(4,1)} %bitcast.458), calls=%async_computation.4 | async-start | bytes 8388608 | tf_op jit(solution)/shard_map/while
  566.7 7.2 slice-start.3
  566.7 10.4 %slice-start.4 = ((s8[4608000]{0:T(1024)(128)(4,1)}), s8[4194304]{0:T(1024)(128)(4,1)S(1)}, s32[]{:S(2)}) async-start(s8[4608000]{0:T(1024)(128)(4,1)} %bitcast.460), calls=%async_computation.6 | async-start | bytes 8388608 | tf_op jit(solution)/shard_map/while
  569.4 7.8 slice-start.5
  573.9 5.9 copy-start.8
  573.9 5.9 copy-start.13
  603.0 20.7 %slice-start = ((s8[4608000]{0:T(1024)(128)(4,1)}), s8[413696]{0:T(1024)(128)(4,1)S(1)}, s32[]{:S(2)}) async-start(s8[4608000]{0:T(1024)(128)(4,1)} %bitcast.456), calls=%async_computation.2 | async-start | bytes 827392 | tf_op jit(solution)/shard_map/while
  609.2 14.5 %slice-start.1 = ((s8[4608000]{0:T(1024)(128)(4,1)}), s8[4194304]{0:T(1024)(128)(4,1)S(1)}, s32[]{:S(2)}) async-start(s8[4608000]{0:T(1024)(128)(4,1)} %bitcast.456), calls=%async_computation.3 | async-start | bytes 8388608 | tf_op jit(solution)/shard_map/while
  632.5 13.7 %copy-start.2 = (f32[4,1,5,5,32,32]{5,1,4,3,2,0:T(1,128)S(1)}, f32[4,1,5,5,32,32]{5,1,4,3,2,0:T(1,128)}, u32[]{:S(2)}) copy-start(f32[4,1,5,5,32,32]{5,1,4,3,2,0:T(1,128)} %fusion.232) | copy-start | bytes 1228804 | tf_op jit(solution)/shard_map/while
  632.5 16.4 %copy-start.7 = (f32[2,9,8,32,32]{3,1,4,2,0:T(8,128)S(1)}, f32[2,9,8,32,32]{3,1,4,2,0:T(8,128)}, u32[]{:S(2)}) copy-start(f32[2,9,8,32,32]{3,1,4,2,0:T(8,128)} %get-tuple-element.914) | copy-start | bytes 1769476 | tf_op jit(solution)/shard_map/while
  632.5 20.9 %slice-start.2 = ((s8[4608000]{0:T(1024)(128)(4,1)}), s8[4194304]{0:T(1024)(128)(4,1)S(1)}, s32[]{:S(2)}) async-start(s8[4608000]{0:T(1024)(128)(4,1)} %bitcast.458), calls=%async_computation.4 | async-start | bytes 8388608 | tf_op jit(solution)/shard_map/while
  646.2 7.2 slice-start.3
  646.2 10.4 %slice-start.4 = ((s8[4608000]{0:T(1024)(128)(4,1)}), s8[4194304]{0:T(1024)(128)(4,1)S(1)}, s32[]{:S(2)}) async-start(s8[4608000]{0:T(1024)(128)(4,1)} %bitcast.460), calls=%async_computation.6 | async-start | bytes 8388608 | tf_op jit(solution)/shard_map/while
  648.9 7.8 slice-start.5
  653.4 5.9 copy-start.8
  653.4 5.9 copy-start.13
  660.2 156.1 %copy-start.1 = (s32[64]{0:T(128)S(1)}, s32[64]{0:T(128)}, u32[]{:S(2)}) copy-start(s32[64]{0:T(128)} %param.25) | copy-start | bytes 772
  (11 other events, 29.4 us)
Sparse Core Ops, SparseCore 0:
  51.5 28.5 all-gather.1
  670.1 144.5 all-reduce.1
where the time goes:
time: 840 us; the launch traced here: 824 us
  local copies, waits for them, and re-layouts  323 us (38%)
  waiting for transfers between devices  177 us (21%)
  matrix products  142 us (17%)
  other arithmetic  88.1 us (10%)
  loops' own time  72.3 us (9%)
  between operations  14.7 us (2%)
    psum x1, waiting for transfers between devices, shards(): summed_all = lax.psum(weight_local, ('lat', 'lon', 'ens'))  144 us
    mul x5, local copies, waits for them, and re-layouts, dense_blocks(): spread = grouped[:, :, :, :, :, :, None, :] * identity[:, None, :, None]  115 us
    another operation x1, loops' own time, shards(): lax.fori_loop(0, panel_count, adjoint_row, jnp.zeros((band_rows + 1, sect...  66.4 us
    dot_general x4, matrix products, forward_row(): jnp.einsum('smpcqo,pq->smpco', block_grad, identity, precision=lax.Precis...  56.4 us
    scatter-add x30, other arithmetic, adjoint_row(): buffer = buffer.at[target_spots[slot]].add(piece)  43.2 us
    concatenate x1, local copies, waits for them, and re-layouts, shards(): jnp.concatenate([whole_band[:, :, whole_band.shape[2] - HW:], whole_band,...  42.8 us
    convert_element_type x2, local copies, waits for them, and re-layouts, dense_blocks(): adjoint_kernel.astype(jnp.bfloat16)  41.1 us
    ppermute x1, waiting for transfers between devices, with_halo(): lax.ppermute(tail, axis, [(i, (i + 1) % count) for i in range(ends)])  29.5 us
  transfers between devices with their start and end apart: 4, of which 3 were waited for; matrix products, arithmetic and copies ran while one was open for 26% of the time, Pallas kernels for 0%

commit v1 on v0

v1 whole, which is shorter than its diff:
```python
import functools
import math

import jax
import jax.numpy as jnp
from jax import lax
from jax.experimental import pallas as pl
from jax.experimental.pallas import tpu as pltpu
from jax.sharding import PartitionSpec as P

MESH = pl.DeviceIdType.MESH
BF16 = jnp.bfloat16
F32 = jnp.float32

C = 256
GW = 32
K = 9
SMAX = 5
WIN = 5
PAD = 16
LW = 128
NB = C // LW
PB = LW // GW
PANEL = 6
TAPS = PANEL * WIN * LW


def chunks_of(cols):
    starts = list(range(0, cols, 256))
    if len(starts) > 1 and cols - starts[-1] < 32:
        starts.pop()
    compute = [(s, (starts[j + 1] if j + 1 < len(starts) else cols) - s) for j, s in enumerate(starts)]
    cuts = [0] + [s + 16 for s in starts[1:]] + [cols]
    send = [(cuts[j], cuts[j + 1] - cuts[j]) for j in range(len(starts))]
    return compute, send


def body(
    lat_n,
    cols,
    fields,
    cot,
    wf,
    wa,
    basis,
    support,
    counts,
    out,
    grad,
    wout,
    xp,
    cp,
    xs,
    cs,
    kf,
    ka,
    cw,
    xt,
    win,
    gbuf,
    tab,
    own_sem,
    row_send,
    row_recv,
    edge_send,
    edge_recv,
):
    compute, send = chunks_of(cols)
    kcols = cw.shape[2]
    lat = lax.axis_index("lat")
    lon = lax.axis_index("lon")
    ens = lax.axis_index("ens")
    sib = 1 - lon
    nlat = lat_n * 2
    top = lat == 0
    bottom = lat == lat_n - 1
    sources = (fields, cot)
    panels = (xp, cp)
    wides = (xs, cs)

    barrier = pltpu.get_barrier_semaphore()
    pl.semaphore_signal(barrier, inc=1, device_id=(lat, sib, ens), device_id_type=MESH)

    @pl.when(jnp.logical_not(top))
    def _():
        for to in (lon, sib):
            pl.semaphore_signal(barrier, inc=1, device_id=(lat - 1, to, ens), device_id_type=MESH)

    @pl.when(jnp.logical_not(bottom))
    def _():
        for to in (lon, sib):
            pl.semaphore_signal(barrier, inc=1, device_id=(lat + 1, to, ens), device_id_type=MESH)

    pl.semaphore_wait(barrier, 5 - 2 * jnp.where(top, 1, 0) - 2 * jnp.where(bottom, 1, 0))

    def own_copy(t, a):
        return pltpu.make_async_copy(
            sources[t].at[a], panels[t].at[2 + a, pl.ds(PAD, cols)], own_sem.at[t, a]
        )

    def target(dirn, a):
        if dirn == 0:
            return (
                jnp.where(top, 0, lat - 1),
                jnp.where(top, sib, lon),
                jnp.where(top, 1 - a, 4 + a),
            )
        return (
            jnp.where(bottom, lat, lat + 1),
            jnp.where(bottom, sib, lon),
            jnp.where(bottom, 5 - a, a),
        )

    def row_copy(t, dirn, a, ch):
        to_lat, to_lon, slot = target(dirn, a)
        start, size = send[ch]
        return pltpu.make_async_remote_copy(
            src_ref=sources[t].at[a, pl.ds(start, size)],
            dst_ref=panels[t].at[slot, pl.ds(PAD + start, size)],
            send_sem=row_send.at[t, dirn, a, ch],
            recv_sem=row_recv.at[t, slot, ch],
            device_id=(to_lat, to_lon, ens),
            device_id_type=MESH,
        )

    def edge_refs(t, a, slot, side):
        src = sources[t].at[a, pl.ds(cols - PAD if side == 0 else 0, PAD)]
        dst = panels[t].at[slot, pl.ds(0 if side == 0 else PAD + cols, PAD)]
        return src, dst

    def edge_copy(t, where_to, a, slot, side, to_lat, to_lon):
        src, dst = edge_refs(t, a, slot, side)
        return pltpu.make_async_remote_copy(
            src_ref=src,
            dst_ref=dst,
            send_sem=edge_send.at[t, where_to, a, side],
            recv_sem=edge_recv.at[t, slot, side],
            device_id=(to_lat, to_lon, ens),
            device_id_type=MESH,
        )

    def edges(t):
        for a in range(2):
            for side in range(2):
                edge_copy(t, 2, a, 2 + a, side, lat, sib).start()
        for dirn, pole in ((0, top), (1, bottom)):
            for a in range(2):
                to_lat, _, slot = target(dirn, a)
                for side in range(2):

                    @pl.when(pole)
                    def _():
                        src, dst = edge_refs(t, a, slot, side)
                        pltpu.make_async_copy(src, dst, edge_recv.at[t, slot, side]).start()

                    @pl.when(jnp.logical_not(pole))
                    def _():
                        edge_copy(t, dirn, a, slot, side, to_lat, sib).start()

    def edges_sent(t):
        for a in range(2):
            for side in range(2):
                edge_copy(t, 2, a, 2 + a, side, lat, sib).wait_send()
        for dirn, pole in ((0, top), (1, bottom)):
            for a in range(2):
                to_lat, _, slot = target(dirn, a)
                for side in range(2):

                    @pl.when(jnp.logical_not(pole))
                    def _():
                        edge_copy(t, dirn, a, slot, side, to_lat, sib).wait_send()

    def wait_edge(t, slot):
        for side in range(2):
            src, dst = edge_refs(t, 0, slot, side)
            pltpu.make_async_copy(dst, dst, edge_recv.at[t, slot, side]).wait()

    def wait_row(t, slot, ch):
        start, size = send[ch]
        dst = panels[t].at[slot, pl.ds(PAD + start, size)]
        pltpu.make_async_copy(dst, dst, row_recv.at[t, slot, ch]).wait()

    for t in range(2):
        for a in range(2):
            own_copy(t, a).start()
    for t in range(2):
        edges(t)
        for ch in range(len(send)):
            for dirn in range(2):
                for a in range(2):
                    row_copy(t, dirn, a, ch).start()

    group_of = lax.broadcasted_iota(jnp.int32, (GW, LW), 1) // GW

    def row_of(virtual):
        mirrored = jnp.logical_or(virtual < 0, virtual >= nlat)
        real = jnp.where(
            virtual < 0, -1 - virtual, jnp.where(virtual >= nlat, 2 * nlat - 1 - virtual, virtual)
        )
        return real, mirrored

    def coefficients(real, offset):
        first = support[real * SMAX] - real
        slot = offset - first
        live = jnp.logical_and(slot >= 0, slot < counts[real])
        slot = jnp.minimum(jnp.maximum(slot, 0), SMAX - 1)
        base = (real * SMAX + slot) * (K * WIN)
        gate = jnp.where(live, 1.0, 0.0).astype(F32)
        return [[basis[base + k * WIN + m] * gate for m in range(WIN)] for k in range(K)]

    def spread(kref, wref, a, p, coef):
        for m0, m1 in ((0, 3), (3, 5)):
            sums = [jnp.zeros((GW, C), F32) for _ in range(m0, m1)]
            for k in range(K):
                wk = wref[k]
                for m in range(m0, m1):
                    sums[m - m0] = sums[m - m0] + coef[k][m] * wk
            for m in range(m0, m1):
                for b in range(NB):
                    part = sums[m - m0][:, b * LW : (b + 1) * LW]
                    for q in range(PB):
                        row = pl.multiple_of(p * (WIN * LW) + m * LW + q * GW, GW)
                        kref[b, pl.ds(row, GW), a * LW : (a + 1) * LW] = jnp.where(
                            group_of == q, part, 0.0
                        ).astype(BF16)

    for a in range(2):
        def forward_offset(q, carry):
            coef = coefficients(lat * 2 + a, q - 2)
            for k in range(K):
                for m in range(WIN):
                    tab[(a * SMAX + q) * (K * WIN) + k * WIN + m] = coef[k][m]
            spread(kf, wf, a, a + q, coef)
            return carry

        def adjoint_offset(q, carry):
            real, mirrored = row_of(lat * 2 - 2 + a + q)
            coef = coefficients(real, jnp.where(mirrored, q - 2, 2 - q))
            spread(ka, wa, a, a + q, coef)
            return carry

        lax.fori_loop(0, SMAX, forward_offset, 0)
        lax.fori_loop(0, SMAX, adjoint_offset, 0)
    for kref in (kf, ka):
        for b in range(NB):
            kref[b, 5 * WIN * LW :, 0:LW] = jnp.zeros((WIN * LW, LW), BF16)
            kref[b, 0 : WIN * LW, LW : 2 * LW] = jnp.zeros((WIN * LW, LW), BF16)

    def widen(t, slot, start, size):
        for b in range(NB):
            wides[t][b, slot, start : start + size, :] = panels[t][
                slot, start : start + size, b * LW : (b + 1) * LW
            ].astype(F32)

    for t in range(2):
        for a in range(2):
            own_copy(t, a).wait()
            wait_edge(t, 2 + a)
            widen(t, 2 + a, 0, cols + 2 * PAD)

    def own_windows(b, carry):
        for m in range(WIN):
            for a in range(2):
                cw[b, m, 0:cols, a * LW : (a + 1) * LW] = cs[
                    b, 2 + a, PAD + 2 - m : PAD + 2 - m + cols, :
                ].astype(BF16)
            if kcols > cols:
                cw[b, m, cols:kcols, :] = jnp.zeros((kcols - cols, 2 * LW), BF16)
        return carry

    lax.fori_loop(0, NB, own_windows, 0)

    def convolve(t, ch, kref, dest, sign):
        start, size = compute[ch]
        for b in range(NB):

            def window_row(p, carry):
                for m in range(WIN):
                    shift = PAD + start + sign * (m - 2)
                    lane = pl.multiple_of(p * (WIN * LW) + m * LW, LW)
                    win[0:size, pl.ds(lane, LW)] = wides[t][
                        b, p, shift : shift + size, :
                    ].astype(BF16)
                return carry

            lax.fori_loop(0, PANEL, window_row, 0)
            res = jnp.dot(win[0:size, :], kref[b], preferred_element_type=F32)
            for a in range(2):
                dest[a, start : start + size, b * LW : (b + 1) * LW] = res[
                    :, a * LW : (a + 1) * LW
                ].astype(BF16)

    def arrive(t, ch):
        start, size = send[ch]
        for slot in (0, 1, 4, 5):
            if ch == 0:
                wait_edge(t, slot)
            wait_row(t, slot, ch)
            lo = 0 if ch == 0 else PAD + start
            hi = PAD + start + size + (PAD if ch == len(send) - 1 else 0)
            widen(t, slot, lo, hi - lo)

    for ch in range(len(compute)):
        arrive(0, ch)
        convolve(0, ch, kf, out, 1)

    def transpose_row(slot, carry):
        for b in range(NB):
            row = pl.multiple_of(slot * LW, LW)
            xt[b, pl.ds(row, LW), 0:cols] = xs[b, slot, PAD : PAD + cols, :].T.astype(BF16)
            if kcols > cols:
                xt[b, pl.ds(row, LW), cols:kcols] = jnp.zeros((LW, kcols - cols), BF16)
        return carry

    lax.fori_loop(0, PANEL, transpose_row, 0)
    wout[...] = jnp.zeros(wout.shape, F32)
    for b in range(NB):

        def weight_offset(m, carry):
            gbuf[...] = jnp.dot(xt[b], cw[b, m], preferred_element_type=F32)
            sums = [wout[k * GW : (k + 1) * GW, b * LW : (b + 1) * LW] for k in range(K)]
            for a in range(2):
                for q in range(SMAX):
                    low = (a + q) * LW
                    part = gbuf[low : low + GW, a * LW : (a + 1) * LW]
                    for g in range(1, PB):
                        part = jnp.where(
                            group_of == g,
                            gbuf[low + g * GW : low + (g + 1) * GW, a * LW : (a + 1) * LW],
                            part,
                        )
                    for k in range(K):
                        sums[k] = sums[k] + tab[(a * SMAX + q) * (K * WIN) + k * WIN + m] * part
            for k in range(K):
                wout[k * GW : (k + 1) * GW, b * LW : (b + 1) * LW] = sums[k]
            return carry

        lax.fori_loop(0, WIN, weight_offset, 0)

    for ch in range(len(compute)):
        arrive(1, ch)
        convolve(1, ch, ka, grad, -1)

    for t in range(2):
        edges_sent(t)
        for ch in range(len(send)):
            for dirn in range(2):
                for a in range(2):
                    row_copy(t, dirn, a, ch).wait_send()


def shards(fields, cotangent, weights, basis_values, support, counts):
    lat_n = lax.axis_size("lat")
    lat = lax.axis_index("lat")
    cols = fields.shape[2]
    kcols = -(-cols // 128) * 128
    n_chunks = len(chunks_of(cols)[0])
    w4 = weights.astype(F32).reshape(K, C // GW, GW, GW)
    wf = jnp.transpose(w4, (0, 3, 1, 2)).reshape(K, GW, C)
    wa = jnp.transpose(w4, (0, 2, 1, 3)).reshape(K, GW, C)
    vmem = pl.BlockSpec(memory_space=pltpu.VMEM)
    smem = pl.BlockSpec(memory_space=pltpu.SMEM)
    hbm = pl.BlockSpec(memory_space=pl.ANY)
    dma = pltpu.SemaphoreType.DMA
    out, grad, wsum = pl.pallas_call(
        functools.partial(body, lat_n, cols),
        out_shape=(
            jax.ShapeDtypeStruct((2, cols, C), BF16),
            jax.ShapeDtypeStruct((2, cols, C), BF16),
            jax.ShapeDtypeStruct((K * GW, C), F32),
        ),
        in_specs=[hbm, hbm, vmem, vmem, smem, smem, smem],
        out_specs=(vmem, vmem, vmem),
        scratch_shapes=[
            pltpu.VMEM((PANEL, cols + 2 * PAD, C), BF16),
            pltpu.VMEM((PANEL, cols + 2 * PAD, C), BF16),
            pltpu.VMEM((NB, PANEL, cols + 2 * PAD, LW), F32),
            pltpu.VMEM((NB, PANEL, cols + 2 * PAD, LW), F32),
            pltpu.VMEM((NB, TAPS, 2 * LW), BF16),
            pltpu.VMEM((NB, TAPS, 2 * LW), BF16),
            pltpu.VMEM((NB, WIN, kcols, 2 * LW), BF16),
            pltpu.VMEM((NB, PANEL * LW, kcols), BF16),
            pltpu.VMEM((256, TAPS), BF16),
            pltpu.VMEM((PANEL * LW, 2 * LW), F32),
            pltpu.SMEM((2 * SMAX * K * WIN,), F32),
            dma((2, 2)),
            dma((2, 2, 2, n_chunks)),
            dma((2, PANEL, n_chunks)),
            dma((2, 3, 2, 2)),
            dma((2, PANEL, 2)),
        ],
        compiler_params=pltpu.CompilerParams(
            collective_id=0, has_side_effects=True, vmem_limit_bytes=56 * 1024 * 1024
        ),
        name="disco",
    )(
        fields[0],
        cotangent[0],
        wf,
        wa,
        basis_values.astype(F32).reshape(-1),
        support.reshape(-1),
        counts,
    )
    total = 2 * lat_n * cols * lax.axis_size("lon") * lax.axis_size("ens") * fields.shape[0]
    wsum = lax.psum(wsum * (1.0 / math.sqrt(total)), ("lat", "lon", "ens")).reshape(K, GW, C)
    share = C // lat_n
    mine = lax.dynamic_slice_in_dim(wsum, lat * share, share, 2)
    return (out[None], grad[None], jnp.transpose(mine, (0, 2, 1)))


def solution(mesh):
    placed = (P("ens", "lat", "lon", None), P("ens", "lat", "lon", None), P(), P(), P(), P())
    return jax.shard_map(
        shards,
        mesh=mesh,
        in_specs=placed,
        out_specs=(
            P("ens", "lat", "lon", None),
            P("ens", "lat", "lon", None),
            P(None, "lat", None),
        ),
        check_vma=False,
    )
```

time: 840 us -> 224 us (0.27); the launches traced: 824 us -> 223 us
  local copies, waits for them, and re-layouts: 323 us -> 11.7 us
  matrix products: 142 us -> 0 us
  other arithmetic: 88.1 us -> 0.99 us
  loops' own time: 72.3 us -> 0 us
  Pallas kernels: 0 us -> 45.3 us
  waiting for transfers between devices: 177 us -> 151 us
    dot_general x27 -> x0, matrix products: 142 us -> none  [the longest x4 56.4 us: forward_row(): jnp.einsum('smpcqo,pq->smpco', block_grad, identity, precision=lax.Precis...]
    mul x6 -> x0, local copies, waits for them, and re-layouts: 117 us -> none  [the longest x5 115 us: dense_blocks(): spread = grouped[:, :, :, :, :, :, None, :] * identity[:, None, :, None]]
    another operation x2 -> x0, loops' own time: 72.3 us -> none  [the longest x1 66.4 us: shards(): lax.fori_loop(0, panel_count, adjoint_row, jnp.zeros((band_rows + 1, sect...]
    convert_element_type x3 -> x0, local copies, waits for them, and re-layouts: 53.2 us -> none  [the longest x2 41.1 us: dense_blocks(): adjoint_kernel.astype(jnp.bfloat16)]
    pallas_call x0 -> x1, Pallas kernels: none -> 45.3 us  [shards(): pl.pallas_call(functools.partial(body, lat_n, cols), out_shape=(jax.Shape...]
    concatenate x9 -> x0, local copies, waits for them, and re-layouts: 43.7 us -> none  [the longest x1 42.8 us: shards(): jnp.concatenate([whole_band[:, :, whole_band.shape[2] - HW:], whole_band,...]
    scatter-add x30 -> x0, other arithmetic: 43.2 us -> none  [adjoint_row(): buffer = buffer.at[target_spots[slot]].add(piece)]
    ppermute x2 -> x0, waiting for transfers between devices: 33.6 us -> none  [the longest x1 29.5 us: with_halo(): lax.ppermute(tail, axis, [(i, (i + 1) % count) for i in range(ends)])]
  transfers between devices with their start and end apart: 4 -> 1, of which waited for: 3 -> 1; matrix products, arithmetic and copies ran while one was open for 26% -> 0% of each run, Pallas kernels for 0% -> 0%
where the time goes in v1:
time: 224 us; the launch traced here: 223 us
  waiting for transfers between devices  151 us (67%)
  Pallas kernels  45.3 us (20%)
  between operations  14.1 us (6%)
  local copies, waits for them, and re-layouts  11.7 us (5%)
    psum x1, waiting for transfers between devices, shards(): lax.psum(wsum * (1.0 / math.sqrt(total)), ('lat', 'lon', 'ens'))  151 us
    pallas_call x1, Pallas kernels, shards(): pl.pallas_call(functools.partial(body, lat_n, cols), out_shape=(jax.Shape...  45.3 us
  transfers between devices with their start and end apart: 1, of which 1 were waited for; matrix products, arithmetic and copies ran while one was open for 0% of the time, Pallas kernels for 0%

profile of v1, /device:TPU:1, one launch (start us, length us, event | category | flops | bytes accessed | tf_op | source)
XLA Modules:
  0.0 223.4 jit_solution(18333751341706994998)
XLA Ops:
  7.2 0.0 all-reduce.2.cloned.1.call-start
  7.2 1.2 reshape.38
  8.5 0.5 copy.11
  9.0 0.0 copy-start.2
  9.0 1.1 reshape.31.wf
  10.0 1.1 reshape.32.wa
  11.1 0.0 copy-done.2
  11.1 1.0 copy.12
  12.1 0.0 copy-start.3
  12.2 1.4 reshape.40.basis
  13.6 0.0 copy-done.3
  13.6 0.1 copy.13
  13.7 0.7 reshape.35.support
  14.4 45.3 %disco.1 = (bf16[2,720,256]{2,1,0:T(8,128)(2,1)}, bf16[2,720,256]{2,1,0:T(8,128)(2,1)}, f32[288,256]{1,0:T(8,128)}) custom-call(bf16[2,720,256]{2,1,0:T(8,128)(2,1)} %bitcast.20, bf16[2,720,256]{2,1,0:T(8,128)(2,1)} %bitcast.21, f32[9,32,256]{2,1,0:T(8,128)} %reshape.31.wf, f32[9,32,256]{2,1,0:T(8,128)} %reshape.32.wa, f32[14400]{0:T(1024)} %reshape.40.basis, ...), custom_call_target="tpu_custom_call" | custom-call | tf_op jit(solution)/shard_map/disco/pallas_call | solution.py:365
  59.7 1.0 broadcast_multiply_fusion
  60.7 0.0 copy-start.1
  60.7 1.4 copy.14
  62.1 0.0 copy-start
  62.1 0.0 all-reduce.2.cloned.1.call-update
  62.1 151.3 %all-reduce.2.cloned.1.call-done = f32[9,32,256]{1,2,0:T(8,128)} async-done(((f32[9,32,256]{1,2,0:T(8,128)}), f32[9,32,256]{1,2,0:T(8,128)}) %all-reduce.2.cloned.1.call-update) | async-done | bytes 294928 | tf_op jit(solution)/shard_map/psum | solution.py:406
  213.5 1.4 dynamic-slice_bitcast_fusion
  214.8 0.0 copy-done.1
  214.8 0.9 copy.18
  215.7 0.0 copy-done
  215.7 0.9 copy.19
Async XLA Ops:
  7.2 206.3 %all-reduce.2.cloned.1.call-start = ((), (), s32[]{:S(2)}) async-start(), calls=%async_computation | async-start | bytes 2359296 | tf_op jit(solution)/shard_map/psum | solution.py:406
  9.0 2.1 copy-start.2
  12.1 1.4 copy-start.3
  60.7 154.2 %copy-start.1 = (bf16[2,720,256]{2,1,0:T(8,128)(2,1)S(1)}, bf16[2,720,256]{2,1,0:T(8,128)(2,1)}, u32[]{:S(2)}) copy-start(bf16[2,720,256]{2,1,0:T(8,128)(2,1)} %get-tuple-element.6) | copy-start | bytes 2211844
  62.1 153.6 %copy-start = (bf16[2,720,256]{2,1,0:T(8,128)(2,1)S(1)}, bf16[2,720,256]{2,1,0:T(8,128)(2,1)}, u32[]{:S(2)}) copy-start(bf16[2,720,256]{2,1,0:T(8,128)(2,1)} %get-tuple-element.7) | copy-start | bytes 2211844
Sparse Core Ops, SparseCore 0:
  62.2 151.1 all-reduce.1

commit v2 on v1

--- a/solution.py
+++ b/solution.py
@@ -38,6 +38,7 @@
 def body(
     lat_n,
     cols,
+    scale,
     fields,
     cot,
     wf,
@@ -59,11 +60,23 @@
     win,
     gbuf,
     tab,
+    wacc,
+    wt,
+    half,
+    quarter,
+    shares,
+    final,
     own_sem,
     row_send,
     row_recv,
     edge_send,
     edge_recv,
+    sum_send,
+    sum_recv,
+    share_send,
+    share_recv,
+    final_send,
+    final_recv,
 ):
     compute, send = chunks_of(cols)
     kcols = cw.shape[2]
@@ -91,7 +104,36 @@
         for to in (lon, sib):
             pl.semaphore_signal(barrier, inc=1, device_id=(lat + 1, to, ens), device_id_type=MESH)
 
-    pl.semaphore_wait(barrier, 5 - 2 * jnp.where(top, 1, 0) - 2 * jnp.where(bottom, 1, 0))
+    mine = lon * 2 + ens
+    n_shares = lat_n // 4
+    share = C // lat_n
+    owner = lax.rem(lat // 8 + lat, 4) == mine
+    partners = ((sib, ens), (lon, 1 - ens), (sib, 1 - ens))
+
+    def share_lat(j):
+        return 4 * j + lax.rem(mine - j // 2 + 4 * lat_n, 4)
+
+    for to_lon, to_ens in partners[1:]:
+        pl.semaphore_signal(barrier, inc=1, device_id=(lat, to_lon, to_ens), device_id_type=MESH)
+
+    @pl.when(owner)
+    def _():
+        def greet(j, carry):
+            pl.semaphore_signal(
+                barrier, inc=1, device_id=(j + jnp.where(j < lat, 0, 1), lon, ens), device_id_type=MESH
+            )
+            return carry
+
+        lax.fori_loop(0, lat_n - 1, greet, 0)
+
+    pl.semaphore_wait(
+        barrier,
+        7
+        + n_shares
+        - jnp.where(owner, 1, 0)
+        - 2 * jnp.where(top, 1, 0)
+        - 2 * jnp.where(bottom, 1, 0),
+    )
 
     def own_copy(t, a):
         return pltpu.make_async_copy(
@@ -300,10 +342,6 @@
             hi = PAD + start + size + (PAD if ch == len(send) - 1 else 0)
             widen(t, slot, lo, hi - lo)
 
-    for ch in range(len(compute)):
-        arrive(0, ch)
-        convolve(0, ch, kf, out, 1)
-
     def transpose_row(slot, carry):
         for b in range(NB):
             row = pl.multiple_of(slot * LW, LW)
@@ -312,13 +350,18 @@
                 xt[b, pl.ds(row, LW), cols:kcols] = jnp.zeros((LW, kcols - cols), BF16)
         return carry
 
-    lax.fori_loop(0, PANEL, transpose_row, 0)
-    wout[...] = jnp.zeros(wout.shape, F32)
+    lax.fori_loop(2, 4, transpose_row, 0)
+    for ch in range(len(compute)):
+        arrive(0, ch)
+    lax.fori_loop(0, 2, transpose_row, 0)
+    lax.fori_loop(4, 6, transpose_row, 0)
+
+    wacc[...] = jnp.zeros(wacc.shape, F32)
     for b in range(NB):
 
         def weight_offset(m, carry):
             gbuf[...] = jnp.dot(xt[b], cw[b, m], preferred_element_type=F32)
-            sums = [wout[k * GW : (k + 1) * GW, b * LW : (b + 1) * LW] for k in range(K)]
+            sums = [wacc[k * GW : (k + 1) * GW, b * LW : (b + 1) * LW] for k in range(K)]
             for a in range(2):
                 for q in range(SMAX):
                     low = (a + q) * LW
@@ -332,14 +375,128 @@
                     for k in range(K):
                         sums[k] = sums[k] + tab[(a * SMAX + q) * (K * WIN) + k * WIN + m] * part
             for k in range(K):
-                wout[k * GW : (k + 1) * GW, b * LW : (b + 1) * LW] = sums[k]
+                wacc[k * GW : (k + 1) * GW, b * LW : (b + 1) * LW] = sums[k]
             return carry
 
         lax.fori_loop(0, WIN, weight_offset, 0)
-
+    for j in range(wacc.shape[0] // LW):
+        turned = wacc[j * LW : (j + 1) * LW, :].T
+        for to in range(lat_n):
+            place = ((to // 8 + to) % 4) * n_shares + to // 4
+            wt[place * share : (place + 1) * share, j * LW : (j + 1) * LW] = turned[
+                to * share : (to + 1) * share
+            ]
+
+    half_rows, quarter_rows = C // 2, C // 4
+
+    def half_copy():
+        return pltpu.make_async_remote_copy(
+            src_ref=wt.at[pl.ds(pl.multiple_of(sib * half_rows, 8), half_rows)],
+            dst_ref=half,
+            send_sem=sum_send.at[0],
+            recv_sem=sum_recv.at[0],
+            device_id=(lat, sib, ens),
+            device_id_type=MESH,
+        )
+
+    def quarter_copy():
+        low = pl.multiple_of(lon * half_rows + (1 - ens) * quarter_rows, 8)
+        return pltpu.make_async_remote_copy(
+            src_ref=wt.at[pl.ds(low, quarter_rows)],
+            dst_ref=quarter,
+            send_sem=sum_send.at[1],
+            recv_sem=sum_recv.at[1],
+            device_id=(lat, lon, 1 - ens),
+            device_id_type=MESH,
+        )
+
+    def share_copy(j):
+        to = share_lat(j)
+        return to, pltpu.make_async_remote_copy(
+            src_ref=wt.at[pl.ds(pl.multiple_of(mine * quarter_rows + j * share, 8), share)],
+            dst_ref=shares.at[jnp.where(lat < to, lat, lat - 1)],
+            send_sem=share_send.at[j],
+            recv_sem=share_recv,
+            device_id=(to, lon, ens),
+            device_id_type=MESH,
+        )
+
+    def final_copy(j):
+        return pltpu.make_async_remote_copy(
+            src_ref=final,
+            dst_ref=final,
+            send_sem=final_send.at[j],
+            recv_sem=final_recv,
+            device_id=(lat, *partners[j]),
+            device_id_type=MESH,
+        )
+
+    def sum_step(step):
+        if step == 0:
+            half_copy().start()
+        elif step == 1:
+            half_copy().wait()
+            low = pl.multiple_of(lon * half_rows, 8)
+            wt[pl.ds(low, half_rows), :] += half[...]
+            quarter_copy().start()
+        elif step == 2:
+            quarter_copy().wait()
+            low = pl.multiple_of(mine * quarter_rows, 8)
+            wt[pl.ds(low, quarter_rows), :] += quarter[...]
+            for j in range(n_shares):
+                to, copy = share_copy(j)
+
+                @pl.when(to != lat)
+                def _():
+                    copy.start()
+
+        elif step == 3:
+
+            @pl.when(owner)
+            def _():
+                pltpu.make_async_copy(shares, shares, share_recv).wait()
+                low = pl.multiple_of(mine * quarter_rows + (lat // 4) * share, 8)
+
+                def add(j, carry):
+                    return carry + shares[j]
+
+                total = lax.fori_loop(0, lat_n - 1, add, wt[pl.ds(low, share), :])
+                final[...] = total * scale
+                for j in range(3):
+                    final_copy(j).start()
+
+        else:
+
+            @pl.when(jnp.logical_not(owner))
+            def _():
+                final_copy(0).wait_recv()
+
+            for k in range(K):
+                wout[k] = final[:, k * GW : (k + 1) * GW]
+
+    sum_step(0)
+    for ch in range(len(compute)):
+        convolve(0, ch, kf, out, 1)
+        if ch < 2:
+            sum_step(ch + 1)
     for ch in range(len(compute)):
         arrive(1, ch)
         convolve(1, ch, ka, grad, -1)
+        if ch == 0:
+            sum_step(3)
+    sum_step(4)
+
+    for j in range(n_shares):
+        to, copy = share_copy(j)
+
+        @pl.when(to != lat)
+        def _():
+            copy.wait_send()
+
+    @pl.when(owner)
+    def _():
+        for j in range(3):
+            final_copy(j).wait_send()
 
     for t in range(2):
         edges_sent(t)
@@ -351,8 +508,10 @@
 
 def shards(fields, cotangent, weights, basis_values, support, counts):
     lat_n = lax.axis_size("lat")
-    lat = lax.axis_index("lat")
     cols = fields.shape[2]
+    share = C // lat_n
+    wcols = -(-K * GW // LW) * LW
+    total = 2 * lat_n * cols * lax.axis_size("lon") * lax.axis_size("ens") * fields.shape[0]
     kcols = -(-cols // 128) * 128
     n_chunks = len(chunks_of(cols)[0])
     w4 = weights.astype(F32).reshape(K, C // GW, GW, GW)
@@ -362,12 +521,12 @@
     smem = pl.BlockSpec(memory_space=pltpu.SMEM)
     hbm = pl.BlockSpec(memory_space=pl.ANY)
     dma = pltpu.SemaphoreType.DMA
-    out, grad, wsum = pl.pallas_call(
-        functools.partial(body, lat_n, cols),
+    out, grad, wgrad = pl.pallas_call(
+        functools.partial(body, lat_n, cols, 1.0 / math.sqrt(total)),
         out_shape=(
             jax.ShapeDtypeStruct((2, cols, C), BF16),
             jax.ShapeDtypeStruct((2, cols, C), BF16),
-            jax.ShapeDtypeStruct((K * GW, C), F32),
+            jax.ShapeDtypeStruct((K, share, GW), F32),
         ),
         in_specs=[hbm, hbm, vmem, vmem, smem, smem, smem],
         out_specs=(vmem, vmem, vmem),
@@ -383,11 +542,23 @@
             pltpu.VMEM((256, TAPS), BF16),
             pltpu.VMEM((PANEL * LW, 2 * LW), F32),
             pltpu.SMEM((2 * SMAX * K * WIN,), F32),
+            pltpu.VMEM((wcols, C), F32),
+            pltpu.VMEM((C, wcols), F32),
+            pltpu.VMEM((C // 2, wcols), F32),
+            pltpu.VMEM((C // 4, wcols), F32),
+            pltpu.VMEM((lat_n - 1, share, wcols), F32),
+            pltpu.VMEM((share, wcols), F32),
             dma((2, 2)),
             dma((2, 2, 2, n_chunks)),
             dma((2, PANEL, n_chunks)),
             dma((2, 3, 2, 2)),
             dma((2, PANEL, 2)),
+            dma((2,)),
+            dma((2,)),
+            dma((lat_n // 4,)),
+            dma,
+            dma((3,)),
+            dma,
         ],
         compiler_params=pltpu.CompilerParams(
             collective_id=0, has_side_effects=True, vmem_limit_bytes=56 * 1024 * 1024
@@ -402,11 +573,7 @@
         support.reshape(-1),
         counts,
     )
-    total = 2 * lat_n * cols * lax.axis_size("lon") * lax.axis_size("ens") * fields.shape[0]
-    wsum = lax.psum(wsum * (1.0 / math.sqrt(total)), ("lat", "lon", "ens")).reshape(K, GW, C)
-    share = C // lat_n
-    mine = lax.dynamic_slice_in_dim(wsum, lat * share, share, 2)
-    return (out[None], grad[None], jnp.transpose(mine, (0, 2, 1)))
+    return (out[None], grad[None], wgrad)
 
 
 def solution(mesh):

time: 224 us -> 71.2 us (0.32)
  the two profiles are of different devices: /device:TPU:1 before, /device:TPU:24 now
where the time goes in v2:
time: 71.2 us; the launch traced here: 71 us
  Pallas kernels  59.5 us (84%)
  local copies, waits for them, and re-layouts  10.7 us (15%)
    pallas_call x1, Pallas kernels, shards(): pl.pallas_call(functools.partial(body, lat_n, cols, 1.0 / math.sqrt(total...  59.5 us
    unnamed x12, local copies, waits for them, and re-layouts  3.69 us
    reshape x2, local copies, waits for them, and re-layouts, shards(): basis_values.astype(F32).reshape(-1)  2.47 us
    reshape x2, local copies, waits for them, and re-layouts, shards(): w4 = weights.astype(F32).reshape(K, C // GW, GW, GW)  1.74 us

profile of v2, /device:TPU:24, one launch (start us, length us, event | category | flops | bytes accessed | tf_op | source)
XLA Modules:
  0.0 71.0 jit_solution(1150527015090910576)
XLA Ops:
  0.6 1.2 %reshape.34 = f32[9,8,32,32]{2,1,3,0:T(8,128)S(1)} reshape(bf16[9,256,32]{1,2,0:T(8,128)(2,1)} %param.8) | data formatting | bytes 442368 | tf_op jit(solution)/shard_map/reshape | solution.py:517
  1.9 0.5 copy.10
  2.4 0.0 copy-start.1
  2.4 1.1 %reshape.29.wa = f32[9,32,256]{2,1,0:T(8,128)} reshape(f32[9,32,8,32]{3,2,1,0:T(8,128)S(1)} %bitcast.13) | data formatting | bytes 589824 | tf_op jit(solution)/shard_map/reshape | solution.py:519
  3.5 1.1 %reshape.28.wf = f32[9,32,256]{2,1,0:T(8,128)} reshape(f32[9,32,8,32]{3,2,1,0:T(8,128)S(1)} %bitcast.12) | data formatting | bytes 589824 | tf_op jit(solution)/shard_map/reshape | solution.py:518
  4.5 0.0 copy-done.1
  4.5 1.0 %copy.11 = f32[64,5,9,5]{3,2,1,0:T(8,128)S(1)} copy(bf16[64,5,9,5]{0,3,2,1:T(8,128)(2,1)S(1)} %copy-done.1) | data formatting | bytes 86400 | tf_op jit(solution)/shard_map/reshape | solution.py:572
  5.6 0.0 copy-start.3
  5.6 1.4 %reshape.36.basis = f32[14400]{0:T(1024)} reshape(f32[64,5,9,5]{3,2,1,0:T(8,128)S(1)} %copy.11) | data formatting | bytes 115200 | tf_op jit(solution)/shard_map/reshape | solution.py:572
  7.0 0.0 copy-done.3
  7.0 0.1 copy.12
  7.1 0.7 %reshape.32.support = s32[320]{0:T(512)} reshape(s32[64,5]{1,0:T(8,128)S(1)} %copy.12) | data formatting | bytes 2560 | tf_op jit(solution)/shard_map/reshape | solution.py:573
  7.8 59.5 %disco.1 = (bf16[2,720,256]{2,1,0:T(8,128)(2,1)}, bf16[2,720,256]{2,1,0:T(8,128)(2,1)}, f32[9,8,32]{2,1,0:T(8,128)}) custom-call(bf16[2,720,256]{2,1,0:T(8,128)(2,1)} %bitcast.16, bf16[2,720,256]{2,1,0:T(8,128)(2,1)} %bitcast.17, f32[9,32,256]{2,1,0:T(8,128)} %reshape.28.wf, f32[9,32,256]{2,1,0:T(8,128)} %reshape.29.wa, f32[14400]{0:T(1024)} %reshape.36.basis, ...), custom_call_target="tpu_custom_call" | custom-call | tf_op jit(solution)/shard_map/disco/pallas_call | solution.py:524
  67.4 0.0 copy-start
  67.4 0.0 copy-start.2
  67.4 2.1 %copy.16 = bf16[1,2,720,256]{3,2,1,0:T(8,128)(2,1)} copy(bf16[1,2,720,256]{3,2,1,0:T(8,128)(2,1)} %bitcast.15) | data formatting | bytes 1474560
  69.5 0.0 copy-done
  69.5 0.9 %copy.17 = bf16[1,2,720,256]{3,2,1,0:T(8,128)(2,1)} copy(bf16[1,2,720,256]{3,2,1,0:T(8,128)(2,1)S(1)} %bitcast.14) | data formatting | bytes 1474560
  70.3 0.0 copy-done.2
  70.4 0.6 copy.18
Async XLA Ops:
  2.4 2.1 %copy-start.1 = (bf16[64,5,9,5]{0,3,2,1:T(8,128)(2,1)S(1)}, bf16[64,5,9,5]{0,3,2,1:T(8,128)(2,1)}, u32[]{:S(2)}) copy-start(bf16[64,5,9,5]{0,3,2,1:T(8,128)(2,1)} %param.9) | copy-start | bytes 86404
  5.6 1.4 %copy-start.3 = (s32[64,5]{0,1:T(8,128)S(1)}, s32[64,5]{0,1:T(8,128)}, u32[]{:S(2)}) copy-start(s32[64,5]{0,1:T(8,128)} %param.10) | copy-start | bytes 3844
  67.4 2.1 %copy-start = (bf16[2,720,256]{2,1,0:T(8,128)(2,1)S(1)}, bf16[2,720,256]{2,1,0:T(8,128)(2,1)}, u32[]{:S(2)}) copy-start(bf16[2,720,256]{2,1,0:T(8,128)(2,1)} %get-tuple-element.7) | copy-start | bytes 2211844
  67.4 3.0 %copy-start.2 = (f32[9,8,32]{2,1,0:T(8,128)S(1)}, f32[9,8,32]{2,1,0:T(8,128)}, u32[]{:S(2)}) copy-start(f32[9,8,32]{2,1,0:T(8,128)} %get-tuple-element.14) | copy-start | bytes 27652

commit v3 on v2

--- a/solution.py
+++ b/solution.py
@@ -41,13 +41,12 @@
     scale,
     fields,
     cot,
-    wf,
-    wa,
-    basis,
-    support,
-    counts,
-    out,
-    grad,
+    weights_hbm,
+    basis_hbm,
+    support_hbm,
+    counts_hbm,
+    out_hbm,
+    grad_hbm,
     wout,
     xp,
     cp,
@@ -57,7 +56,16 @@
     ka,
     cw,
     xt,
-    win,
+    out,
+    grad,
+    wf,
+    wa,
+    weights,
+    basis_in,
+    support,
+    counts,
+    basis_wide,
+    basis,
     gbuf,
     tab,
     wacc,
@@ -66,6 +74,9 @@
     quarter,
     shares,
     final,
+    basis_sem,
+    arg_sem,
+    out_sem,
     own_sem,
     row_send,
     row_recv,
@@ -222,15 +233,50 @@
         dst = panels[t].at[slot, pl.ds(PAD + start, size)]
         pltpu.make_async_copy(dst, dst, row_recv.at[t, slot, ch]).wait()
 
+    def send_rows(t, ch, a):
+        for dirn in range(2):
+            row_copy(t, dirn, a, ch).start()
+
+    n_chunks = len(send)
+    for t in range(2):
+        edges(t)
+        for ch in range(n_chunks if t == 0 else 1):
+            for a in range(2):
+                send_rows(t, ch, a)
+    small = [
+        pltpu.make_async_copy(src, dst, arg_sem.at[j])
+        for j, (src, dst) in enumerate(
+            (
+                (basis_hbm, basis_in),
+                (support_hbm, support),
+                (counts_hbm, counts),
+                (weights_hbm, weights),
+            )
+        )
+    ]
+    for copy in small:
+        copy.start()
     for t in range(2):
         for a in range(2):
             own_copy(t, a).start()
-    for t in range(2):
-        edges(t)
-        for ch in range(len(send)):
-            for dirn in range(2):
-                for a in range(2):
-                    row_copy(t, dirn, a, ch).start()
+    later = [(ch, a) for ch in range(1, n_chunks) for a in range(2)]
+
+    def send_later(count):
+        for _ in range(min(count, len(later))):
+            send_rows(1, *later.pop(0))
+
+    small[0].wait()
+    basis_wide[...] = basis_in[...].astype(F32)
+    basis_copy = pltpu.make_async_copy(basis_wide, basis, basis_sem)
+    basis_copy.start()
+    for copy in small[1:]:
+        copy.wait()
+    for k in range(K):
+        wide = weights[k].astype(F32)
+        wf[k] = wide
+        turned = wide.T
+        wa[k] = jnp.concatenate([turned[g * GW : (g + 1) * GW] for g in range(C // GW)], axis=1)
+    basis_copy.wait()
 
     group_of = lax.broadcasted_iota(jnp.int32, (GW, LW), 1) // GW
 
@@ -242,13 +288,12 @@
         return real, mirrored
 
     def coefficients(real, offset):
-        first = support[real * SMAX] - real
+        first = support[0, real] - real
         slot = offset - first
         live = jnp.logical_and(slot >= 0, slot < counts[real])
         slot = jnp.minimum(jnp.maximum(slot, 0), SMAX - 1)
-        base = (real * SMAX + slot) * (K * WIN)
         gate = jnp.where(live, 1.0, 0.0).astype(F32)
-        return [[basis[base + k * WIN + m] * gate for m in range(WIN)] for k in range(K)]
+        return [[basis[slot, k, m, real] * gate for m in range(WIN)] for k in range(K)]
 
     def spread(kref, wref, a, p, coef):
         for m0, m1 in ((0, 3), (3, 5)):
@@ -312,25 +357,35 @@
 
     lax.fori_loop(0, NB, own_windows, 0)
 
+    def out_copy(t, ch):
+        cells = pl.ds(compute[ch][0], compute[ch][1])
+        return pltpu.make_async_copy(
+            (out, grad)[t].at[:, cells], (out_hbm, grad_hbm)[t].at[:, cells], out_sem.at[t, ch]
+        )
+
     def convolve(t, ch, kref, dest, sign):
         start, size = compute[ch]
         for b in range(NB):
 
-            def window_row(p, carry):
-                for m in range(WIN):
-                    shift = PAD + start + sign * (m - 2)
-                    lane = pl.multiple_of(p * (WIN * LW) + m * LW, LW)
-                    win[0:size, pl.ds(lane, LW)] = wides[t][
-                        b, p, shift : shift + size, :
+            window = jnp.concatenate(
+                [
+                    wides[t][
+                        b,
+                        p,
+                        PAD + start + sign * (m - 2) : PAD + start + sign * (m - 2) + size,
+                        :,
                     ].astype(BF16)
-                return carry
-
-            lax.fori_loop(0, PANEL, window_row, 0)
-            res = jnp.dot(win[0:size, :], kref[b], preferred_element_type=F32)
+                    for p in range(PANEL)
+                    for m in range(WIN)
+                ],
+                axis=1,
+            )
+            res = jnp.dot(window, kref[b], preferred_element_type=F32)
             for a in range(2):
                 dest[a, start : start + size, b * LW : (b + 1) * LW] = res[
                     :, a * LW : (a + 1) * LW
                 ].astype(BF16)
+        out_copy(t, ch).start()
 
     def arrive(t, ch):
         start, size = send[ch]
@@ -344,41 +399,55 @@
 
     def transpose_row(slot, carry):
         for b in range(NB):
-            row = pl.multiple_of(slot * LW, LW)
+            row = pl.multiple_of(jnp.where(slot < 2, slot + 2, jnp.where(slot < 4, slot - 2, slot)) * LW, LW)
             xt[b, pl.ds(row, LW), 0:cols] = xs[b, slot, PAD : PAD + cols, :].T.astype(BF16)
             if kcols > cols:
                 xt[b, pl.ds(row, LW), cols:kcols] = jnp.zeros((LW, kcols - cols), BF16)
         return carry
 
+    places = {2: 0, 3: 1, 0: 2, 1: 3, 4: 4, 5: 5}
+    wacc[...] = jnp.zeros(wacc.shape, F32)
+
+    def weight_gradient(lo, hi):
+        for b in range(NB):
+
+            def weight_offset(m, carry):
+                gbuf[lo * LW : hi * LW, :] = jnp.dot(
+                    xt[b, lo * LW : hi * LW, :], cw[b, m], preferred_element_type=F32
+                )
+                sums = [wacc[k * GW : (k + 1) * GW, b * LW : (b + 1) * LW] for k in range(K)]
+                for a in range(2):
+                    for q in range(SMAX):
+                        if not lo <= places[a + q] < hi:
+                            continue
+                        low = places[a + q] * LW
+                        part = gbuf[low : low + GW, a * LW : (a + 1) * LW]
+                        for g in range(1, PB):
+                            part = jnp.where(
+                                group_of == g,
+                                gbuf[low + g * GW : low + (g + 1) * GW, a * LW : (a + 1) * LW],
+                                part,
+                            )
+                        for k in range(K):
+                            sums[k] = (
+                                sums[k] + tab[(a * SMAX + q) * (K * WIN) + k * WIN + m] * part
+                            )
+                for k in range(K):
+                    wacc[k * GW : (k + 1) * GW, b * LW : (b + 1) * LW] = sums[k]
+                return carry
+
+            lax.fori_loop(0, WIN, weight_offset, 0)
+
     lax.fori_loop(2, 4, transpose_row, 0)
-    for ch in range(len(compute)):
+    weight_gradient(0, 2)
+    last = len(compute) - 1
+    for ch in range(last):
         arrive(0, ch)
+        convolve(0, ch, kf, out, 1)
+    arrive(0, last)
     lax.fori_loop(0, 2, transpose_row, 0)
     lax.fori_loop(4, 6, transpose_row, 0)
-
-    wacc[...] = jnp.zeros(wacc.shape, F32)
-    for b in range(NB):
-
-        def weight_offset(m, carry):
-            gbuf[...] = jnp.dot(xt[b], cw[b, m], preferred_element_type=F32)
-            sums = [wacc[k * GW : (k + 1) * GW, b * LW : (b + 1) * LW] for k in range(K)]
-            for a in range(2):
-                for q in range(SMAX):
-                    low = (a + q) * LW
-                    part = gbuf[low : low + GW, a * LW : (a + 1) * LW]
-                    for g in range(1, PB):
-                        part = jnp.where(
-                            group_of == g,
-                            gbuf[low + g * GW : low + (g + 1) * GW, a * LW : (a + 1) * LW],
-                            part,
-                        )
-                    for k in range(K):
-                        sums[k] = sums[k] + tab[(a * SMAX + q) * (K * WIN) + k * WIN + m] * part
-            for k in range(K):
-                wacc[k * GW : (k + 1) * GW, b * LW : (b + 1) * LW] = sums[k]
-            return carry
-
-        lax.fori_loop(0, WIN, weight_offset, 0)
+    weight_gradient(2, 6)
     for j in range(wacc.shape[0] // LW):
         turned = wacc[j * LW : (j + 1) * LW, :].T
         for to in range(lat_n):
@@ -475,14 +544,19 @@
                 wout[k] = final[:, k * GW : (k + 1) * GW]
 
     sum_step(0)
+    send_later(1)
+    convolve(0, last, kf, out, 1)
+    sum_step(1)
+    send_later(1)
     for ch in range(len(compute)):
-        convolve(0, ch, kf, out, 1)
-        if ch < 2:
-            sum_step(ch + 1)
-    for ch in range(len(compute)):
+        if ch == last:
+            send_later(len(later))
         arrive(1, ch)
         convolve(1, ch, ka, grad, -1)
         if ch == 0:
+            sum_step(2)
+            send_later(1)
+        if ch == max(last - 1, 0):
             sum_step(3)
     sum_step(4)
 
@@ -499,11 +573,35 @@
             final_copy(j).wait_send()
 
     for t in range(2):
+        for ch in range(len(compute)):
+            out_copy(t, ch).wait()
         edges_sent(t)
         for ch in range(len(send)):
             for dirn in range(2):
                 for a in range(2):
                     row_copy(t, dirn, a, ch).wait_send()
+
+
+def store(pieces, *refs):
+    parts = []
+    for j in range(3):
+        src, dst, held = refs[j], refs[3 + j], refs[6 + j]
+        size = src.shape[1] // pieces if j < 2 else src.shape[1]
+        for n in range(pieces if j < 2 else 1):
+            cells = (slice(None), pl.ds(n * size, size))
+            parts.append(
+                (
+                    pltpu.make_async_copy(src.at[cells], held.at[cells], refs[9].at[j, n]),
+                    pltpu.make_async_copy(held.at[cells], dst.at[cells], refs[10].at[j, n]),
+                )
+            )
+    for bring, _ in parts:
+        bring.start()
+    for bring, take in parts:
+        bring.wait()
+        take.start()
+    for _, take in parts:
+        take.wait()
 
 
 def shards(fields, cotangent, weights, basis_values, support, counts):
@@ -514,12 +612,7 @@
     total = 2 * lat_n * cols * lax.axis_size("lon") * lax.axis_size("ens") * fields.shape[0]
     kcols = -(-cols // 128) * 128
     n_chunks = len(chunks_of(cols)[0])
-    w4 = weights.astype(F32).reshape(K, C // GW, GW, GW)
-    wf = jnp.transpose(w4, (0, 3, 1, 2)).reshape(K, GW, C)
-    wa = jnp.transpose(w4, (0, 2, 1, 3)).reshape(K, GW, C)
-    vmem = pl.BlockSpec(memory_space=pltpu.VMEM)
-    smem = pl.BlockSpec(memory_space=pltpu.SMEM)
-    hbm = pl.BlockSpec(memory_space=pl.ANY)
+    anywhere = pl.BlockSpec(memory_space=pl.ANY)
     dma = pltpu.SemaphoreType.DMA
     out, grad, wgrad = pl.pallas_call(
         functools.partial(body, lat_n, cols, 1.0 / math.sqrt(total)),
@@ -528,8 +621,8 @@
             jax.ShapeDtypeStruct((2, cols, C), BF16),
             jax.ShapeDtypeStruct((K, share, GW), F32),
         ),
-        in_specs=[hbm, hbm, vmem, vmem, smem, smem, smem],
-        out_specs=(vmem, vmem, vmem),
+        in_specs=[pl.BlockSpec(memory_space=pltpu.HBM)] * 6,
+        out_specs=(anywhere, anywhere, pl.BlockSpec(memory_space=pltpu.VMEM)),
         scratch_shapes=[
             pltpu.VMEM((PANEL, cols + 2 * PAD, C), BF16),
             pltpu.VMEM((PANEL, cols + 2 * PAD, C), BF16),
@@ -539,7 +632,16 @@
             pltpu.VMEM((NB, TAPS, 2 * LW), BF16),
             pltpu.VMEM((NB, WIN, kcols, 2 * LW), BF16),
             pltpu.VMEM((NB, PANEL * LW, kcols), BF16),
-            pltpu.VMEM((256, TAPS), BF16),
+            pltpu.VMEM((2, cols, C), BF16),
+            pltpu.VMEM((2, cols, C), BF16),
+            pltpu.VMEM((K, GW, C), F32),
+            pltpu.VMEM((K, GW, C), F32),
+            pltpu.VMEM((K, GW, C), BF16),
+            pltpu.VMEM((SMAX, K, WIN, 2 * lat_n), BF16),
+            pltpu.SMEM((SMAX, 2 * lat_n), jnp.int32),
+            pltpu.SMEM((2 * lat_n,), jnp.int32),
+            pltpu.VMEM((SMAX, K, WIN, 2 * lat_n), F32),
+            pltpu.SMEM((SMAX, K, WIN, 2 * lat_n), F32),
             pltpu.VMEM((PANEL * LW, 2 * LW), F32),
             pltpu.SMEM((2 * SMAX * K * WIN,), F32),
             pltpu.VMEM((wcols, C), F32),
@@ -548,6 +650,9 @@
             pltpu.VMEM((C // 4, wcols), F32),
             pltpu.VMEM((lat_n - 1, share, wcols), F32),
             pltpu.VMEM((share, wcols), F32),
+            dma,
+            dma((4,)),
+            dma((2, n_chunks)),
             dma((2, 2)),
             dma((2, 2, 2, n_chunks)),
             dma((2, PANEL, n_chunks)),
@@ -561,18 +666,33 @@
             dma,
         ],
         compiler_params=pltpu.CompilerParams(
-            collective_id=0, has_side_effects=True, vmem_limit_bytes=56 * 1024 * 1024
+            collective_id=0, has_side_effects=True, vmem_limit_bytes=61 * 1024 * 1024
         ),
         name="disco",
     )(
         fields[0],
         cotangent[0],
-        wf,
-        wa,
-        basis_values.astype(F32).reshape(-1),
-        support.reshape(-1),
+        jnp.transpose(weights, (0, 2, 1)),
+        jnp.transpose(basis_values, (1, 2, 3, 0)),
+        jnp.transpose(support),
         counts,
     )
+    pieces = 3
+    out, grad, wgrad = pl.pallas_call(
+        functools.partial(store, pieces),
+        out_shape=[jax.ShapeDtypeStruct(o.shape, o.dtype) for o in (out, grad, wgrad)],
+        in_specs=[anywhere] * 3,
+        out_specs=[anywhere] * 3,
+        scratch_shapes=[
+            pltpu.VMEM(out.shape, BF16),
+            pltpu.VMEM(grad.shape, BF16),
+            pltpu.VMEM(wgrad.shape, F32),
+            dma((3, pieces)),
+            dma((3, pieces)),
+        ],
+        compiler_params=pltpu.CompilerParams(vmem_limit_bytes=61 * 1024 * 1024),
+        name="store",
+    )(out, grad, wgrad)
     return (out[None], grad[None], wgrad)
 
 

time: 71.2 us -> 59.4 us (0.83)
  the two profiles are of different devices: /device:TPU:24 before, /device:TPU:10 now
where the time goes in v3:
time: 59.4 us; the launch traced here: 59.2 us
  Pallas kernels  58.6 us (99%)
  between operations  0.64 us (1%)
    pallas_call x1, Pallas kernels, shards(): pl.pallas_call(functools.partial(body, lat_n, cols, 1.0 / math.sqrt(total...  56.3 us
    pallas_call x1, Pallas kernels, shards(): pl.pallas_call(functools.partial(store, pieces), out_shape=[jax.ShapeDtyp...  2.33 us

profile of v3, /device:TPU:10, one launch (start us, length us, event | category | flops | bytes accessed | tf_op | source)
XLA Modules:
  0.0 59.2 jit_solution(7477152827779979895)
XLA Ops:
  0.6 56.3 %disco.1 = (bf16[2,720,256]{2,1,0:T(8,128)(2,1)}, bf16[2,720,256]{2,1,0:T(8,128)(2,1)}, f32[9,8,32]{2,1,0:T(8,128)}) custom-call(bf16[2,720,256]{2,1,0:T(8,128)(2,1)} %bitcast.7, bf16[2,720,256]{2,1,0:T(8,128)(2,1)} %bitcast.8, bf16[9,32,256]{2,1,0:T(8,128)(2,1)} %bitcast.9, bf16[5,9,5,64]{3,2,1,0:T(8,128)(2,1)} %bitcast.10, s32[5,64]{1,0:T(8,128)} %bitcast.11, ...), custom_call_target="tpu_custom_call" | custom-call | tf_op jit(solution)/shard_map/disco/pallas_call | solution.py:617
  56.9 2.3 %store.1 = (bf16[2,720,256]{2,1,0:T(8,128)(2,1)}, bf16[2,720,256]{2,1,0:T(8,128)(2,1)}, f32[9,8,32]{2,1,0:T(8,128)}) custom-call(bf16[2,720,256]{2,1,0:T(8,128)(2,1)} %get-tuple-element.9.refs_0_, bf16[2,720,256]{2,1,0:T(8,128)(2,1)} %get-tuple-element.10.refs_1_, f32[9,8,32]{2,1,0:T(8,128)} %get-tuple-element.11.refs_2_), custom_call_target="tpu_custom_call" | custom-call | tf_op jit(solution)/shard_map/store/pallas_call | solution.py:681

commit v4 on v3

--- a/solution.py
+++ b/solution.py
@@ -22,17 +22,24 @@
 NB = C // LW
 PB = LW // GW
 PANEL = 6
+WIDTHS = (256, 304)
+EARLY = 3
+PACE = (1, 1, 1)
 TAPS = PANEL * WIN * LW
 
 
-def chunks_of(cols):
-    starts = list(range(0, cols, 256))
+def chunks_of(cols, width):
+    starts = list(range(0, cols, width))
     if len(starts) > 1 and cols - starts[-1] < 32:
         starts.pop()
     compute = [(s, (starts[j + 1] if j + 1 < len(starts) else cols) - s) for j, s in enumerate(starts)]
     cuts = [0] + [s + 16 for s in starts[1:]] + [cols]
     send = [(cuts[j], cuts[j + 1] - cuts[j]) for j in range(len(starts))]
-    return compute, send
+    pieces = []
+    for start, size in send:
+        first = -(-size // 32) * 16
+        pieces.append([(start, first), (start + first, size - first)])
+    return compute, pieces
 
 
 def body(
@@ -71,7 +78,6 @@
     wacc,
     wt,
     half,
-    quarter,
     shares,
     final,
     basis_sem,
@@ -89,7 +95,7 @@
     final_send,
     final_recv,
 ):
-    compute, send = chunks_of(cols)
+    computes, sends = zip(*(chunks_of(cols, width) for width in WIDTHS))
     kcols = cw.shape[2]
     lat = lax.axis_index("lat")
     lon = lax.axis_index("lon")
@@ -115,14 +121,13 @@
         for to in (lon, sib):
             pl.semaphore_signal(barrier, inc=1, device_id=(lat + 1, to, ens), device_id_type=MESH)
 
-    mine = lon * 2 + ens
-    n_shares = lat_n // 4
+    n_shares = lat_n // 2
     share = C // lat_n
-    owner = lax.rem(lat // 8 + lat, 4) == mine
+    owner = lax.rem(lat // 8 + lat, 2) == lon
     partners = ((sib, ens), (lon, 1 - ens), (sib, 1 - ens))
 
     def share_lat(j):
-        return 4 * j + lax.rem(mine - j // 2 + 4 * lat_n, 4)
+        return 2 * j + lax.rem(lon + j // 4, 2)
 
     for to_lon, to_ens in partners[1:]:
         pl.semaphore_signal(barrier, inc=1, device_id=(lat, to_lon, to_ens), device_id_type=MESH)
@@ -164,14 +169,14 @@
             jnp.where(bottom, 5 - a, a),
         )
 
-    def row_copy(t, dirn, a, ch):
+    def row_copy(t, dirn, a, ch, h):
         to_lat, to_lon, slot = target(dirn, a)
-        start, size = send[ch]
+        start, size = sends[t][ch][h]
         return pltpu.make_async_remote_copy(
             src_ref=sources[t].at[a, pl.ds(start, size)],
             dst_ref=panels[t].at[slot, pl.ds(PAD + start, size)],
-            send_sem=row_send.at[t, dirn, a, ch],
-            recv_sem=row_recv.at[t, slot, ch],
+            send_sem=row_send.at[t, dirn, a, ch, h],
+            recv_sem=row_recv.at[t, slot, ch, h],
             device_id=(to_lat, to_lon, ens),
             device_id_type=MESH,
         )
@@ -229,20 +234,21 @@
             pltpu.make_async_copy(dst, dst, edge_recv.at[t, slot, side]).wait()
 
     def wait_row(t, slot, ch):
-        start, size = send[ch]
-        dst = panels[t].at[slot, pl.ds(PAD + start, size)]
-        pltpu.make_async_copy(dst, dst, row_recv.at[t, slot, ch]).wait()
-
-    def send_rows(t, ch, a):
-        for dirn in range(2):
-            row_copy(t, dirn, a, ch).start()
-
-    n_chunks = len(send)
+        for h in range(2):
+            start, size = sends[t][ch][h]
+            dst = panels[t].at[slot, pl.ds(PAD + start, size)]
+            pltpu.make_async_copy(dst, dst, row_recv.at[t, slot, ch, h]).wait()
+
+    def send_rows(t, ch, h):
+        for a in range(2):
+            for dirn in range(2):
+                row_copy(t, dirn, a, ch, h).start()
+
+    orders = [[(ch, h) for ch in range(len(send)) for h in range(2)] for send in sends]
     for t in range(2):
         edges(t)
-        for ch in range(n_chunks if t == 0 else 1):
-            for a in range(2):
-                send_rows(t, ch, a)
+        for ch, h in orders[0] if t == 0 else orders[1][:EARLY]:
+            send_rows(t, ch, h)
     small = [
         pltpu.make_async_copy(src, dst, arg_sem.at[j])
         for j, (src, dst) in enumerate(
@@ -259,7 +265,7 @@
     for t in range(2):
         for a in range(2):
             own_copy(t, a).start()
-    later = [(ch, a) for ch in range(1, n_chunks) for a in range(2)]
+    later = orders[1][EARLY:]
 
     def send_later(count):
         for _ in range(min(count, len(later))):
@@ -358,13 +364,13 @@
     lax.fori_loop(0, NB, own_windows, 0)
 
     def out_copy(t, ch):
-        cells = pl.ds(compute[ch][0], compute[ch][1])
+        cells = pl.ds(*computes[t][ch])
         return pltpu.make_async_copy(
             (out, grad)[t].at[:, cells], (out_hbm, grad_hbm)[t].at[:, cells], out_sem.at[t, ch]
         )
 
     def convolve(t, ch, kref, dest, sign):
-        start, size = compute[ch]
+        start, size = computes[t][ch]
         for b in range(NB):
 
             window = jnp.concatenate(
@@ -388,7 +394,8 @@
         out_copy(t, ch).start()
 
     def arrive(t, ch):
-        start, size = send[ch]
+        send = sends[t]
+        start, size = send[ch][0][0], send[ch][0][1] + send[ch][1][1]
         for slot in (0, 1, 4, 5):
             if ch == 0:
                 wait_edge(t, slot)
@@ -397,23 +404,31 @@
             hi = PAD + start + size + (PAD if ch == len(send) - 1 else 0)
             widen(t, slot, lo, hi - lo)
 
-    def transpose_row(slot, carry):
-        for b in range(NB):
-            row = pl.multiple_of(jnp.where(slot < 2, slot + 2, jnp.where(slot < 4, slot - 2, slot)) * LW, LW)
-            xt[b, pl.ds(row, LW), 0:cols] = xs[b, slot, PAD : PAD + cols, :].T.astype(BF16)
-            if kcols > cols:
-                xt[b, pl.ds(row, LW), cols:kcols] = jnp.zeros((LW, kcols - cols), BF16)
-        return carry
+    def transpose_rows(slots, start, end):
+        def transpose_row(slot, carry):
+            for b in range(NB):
+                place = jnp.where(slot < 2, slot + 2, jnp.where(slot < 4, slot - 2, slot))
+                row = pl.multiple_of(place * LW, LW)
+                xt[b, pl.ds(row, LW), start:end] = xs[
+                    b, slot, PAD + start : PAD + end, :
+                ].T.astype(BF16)
+                if end == cols and kcols > cols:
+                    xt[b, pl.ds(row, LW), cols:kcols] = jnp.zeros((LW, kcols - cols), BF16)
+            return carry
+
+        lax.fori_loop(*slots, transpose_row, 0)
 
     places = {2: 0, 3: 1, 0: 2, 1: 3, 4: 4, 5: 5}
     wacc[...] = jnp.zeros(wacc.shape, F32)
 
-    def weight_gradient(lo, hi):
+    def weight_gradient(lo, hi, start, end):
         for b in range(NB):
 
             def weight_offset(m, carry):
                 gbuf[lo * LW : hi * LW, :] = jnp.dot(
-                    xt[b, lo * LW : hi * LW, :], cw[b, m], preferred_element_type=F32
+                    xt[b, lo * LW : hi * LW, start:end],
+                    cw[b, m, start:end],
+                    preferred_element_type=F32
                 )
                 sums = [wacc[k * GW : (k + 1) * GW, b * LW : (b + 1) * LW] for k in range(K)]
                 for a in range(2):
@@ -438,25 +453,27 @@
 
             lax.fori_loop(0, WIN, weight_offset, 0)
 
-    lax.fori_loop(2, 4, transpose_row, 0)
-    weight_gradient(0, 2)
+    transpose_rows((2, 4), 0, cols)
+    weight_gradient(0, 2, 0, kcols)
+    compute = computes[0]
     last = len(compute) - 1
-    for ch in range(last):
+    for ch in range(len(compute)):
         arrive(0, ch)
-        convolve(0, ch, kf, out, 1)
-    arrive(0, last)
-    lax.fori_loop(0, 2, transpose_row, 0)
-    lax.fori_loop(4, 6, transpose_row, 0)
-    weight_gradient(2, 6)
+        start, end = compute[ch][0], compute[ch][0] + compute[ch][1]
+        for slots in ((0, 2), (4, 6)):
+            transpose_rows(slots, start, end)
+        weight_gradient(2, 6, start, kcols if ch == last else end)
+        if ch < last:
+            convolve(0, ch, kf, out, 1)
     for j in range(wacc.shape[0] // LW):
         turned = wacc[j * LW : (j + 1) * LW, :].T
         for to in range(lat_n):
-            place = ((to // 8 + to) % 4) * n_shares + to // 4
+            place = ((to // 8 + to) % 2) * n_shares + to // 2
             wt[place * share : (place + 1) * share, j * LW : (j + 1) * LW] = turned[
                 to * share : (to + 1) * share
             ]
 
-    half_rows, quarter_rows = C // 2, C // 4
+    half_rows = C // 2
 
     def half_copy():
         return pltpu.make_async_remote_copy(
@@ -468,21 +485,10 @@
             device_id_type=MESH,
         )
 
-    def quarter_copy():
-        low = pl.multiple_of(lon * half_rows + (1 - ens) * quarter_rows, 8)
-        return pltpu.make_async_remote_copy(
-            src_ref=wt.at[pl.ds(low, quarter_rows)],
-            dst_ref=quarter,
-            send_sem=sum_send.at[1],
-            recv_sem=sum_recv.at[1],
-            device_id=(lat, lon, 1 - ens),
-            device_id_type=MESH,
-        )
-
     def share_copy(j):
         to = share_lat(j)
         return to, pltpu.make_async_remote_copy(
-            src_ref=wt.at[pl.ds(pl.multiple_of(mine * quarter_rows + j * share, 8), share)],
+            src_ref=wt.at[pl.ds(pl.multiple_of(lon * half_rows + j * share, 8), share)],
             dst_ref=shares.at[jnp.where(lat < to, lat, lat - 1)],
             send_sem=share_send.at[j],
             recv_sem=share_recv,
@@ -492,10 +498,10 @@
 
     def final_copy(j):
         return pltpu.make_async_remote_copy(
-            src_ref=final,
-            dst_ref=final,
+            src_ref=final.at[ens],
+            dst_ref=final.at[ens],
             send_sem=final_send.at[j],
-            recv_sem=final_recv,
+            recv_sem=final_recv.at[ens],
             device_id=(lat, *partners[j]),
             device_id_type=MESH,
         )
@@ -507,11 +513,6 @@
             half_copy().wait()
             low = pl.multiple_of(lon * half_rows, 8)
             wt[pl.ds(low, half_rows), :] += half[...]
-            quarter_copy().start()
-        elif step == 2:
-            quarter_copy().wait()
-            low = pl.multiple_of(mine * quarter_rows, 8)
-            wt[pl.ds(low, quarter_rows), :] += quarter[...]
             for j in range(n_shares):
                 to, copy = share_copy(j)
 
@@ -519,46 +520,47 @@
                 def _():
                     copy.start()
 
-        elif step == 3:
+        elif step == 2:
 
             @pl.when(owner)
             def _():
                 pltpu.make_async_copy(shares, shares, share_recv).wait()
-                low = pl.multiple_of(mine * quarter_rows + (lat // 4) * share, 8)
+                low = pl.multiple_of(lon * half_rows + (lat // 2) * share, 8)
 
                 def add(j, carry):
                     return carry + shares[j]
 
-                total = lax.fori_loop(0, lat_n - 1, add, wt[pl.ds(low, share), :])
-                final[...] = total * scale
+                final[ens] = lax.fori_loop(0, lat_n - 1, add, wt[pl.ds(low, share), :])
                 for j in range(3):
                     final_copy(j).start()
 
         else:
-
-            @pl.when(jnp.logical_not(owner))
-            def _():
-                final_copy(0).wait_recv()
-
+            for e in range(2):
+
+                @pl.when(jnp.logical_not(jnp.logical_and(owner, ens == e)))
+                def _():
+                    part = final.at[e]
+                    pltpu.make_async_copy(part, part, final_recv.at[e]).wait()
+
+            total = (final[0] + final[1]) * scale
             for k in range(K):
-                wout[k] = final[:, k * GW : (k + 1) * GW]
+                wout[k] = total[:, k * GW : (k + 1) * GW]
 
     sum_step(0)
-    send_later(1)
+    send_later(PACE[0])
     convolve(0, last, kf, out, 1)
     sum_step(1)
-    send_later(1)
-    for ch in range(len(compute)):
-        if ch == last:
-            send_later(len(later))
+    send_later(PACE[1])
+    last = len(computes[1]) - 1
+    for ch in range(last + 1):
+        send_later(len([c for c, _ in later if c <= ch]))
         arrive(1, ch)
         convolve(1, ch, ka, grad, -1)
         if ch == 0:
+            send_later(PACE[2])
+        if ch == max(last - 1, 0):
             sum_step(2)
-            send_later(1)
-        if ch == max(last - 1, 0):
-            sum_step(3)
-    sum_step(4)
+    sum_step(3)
 
     for j in range(n_shares):
         to, copy = share_copy(j)
@@ -573,13 +575,14 @@
             final_copy(j).wait_send()
 
     for t in range(2):
-        for ch in range(len(compute)):
+        for ch in range(len(computes[t])):
             out_copy(t, ch).wait()
         edges_sent(t)
-        for ch in range(len(send)):
+        for ch in range(len(sends[t])):
             for dirn in range(2):
                 for a in range(2):
-                    row_copy(t, dirn, a, ch).wait_send()
+                    for h in range(2):
+                        row_copy(t, dirn, a, ch, h).wait_send()
 
 
 def store(pieces, *refs):
@@ -611,7 +614,7 @@
     wcols = -(-K * GW // LW) * LW
     total = 2 * lat_n * cols * lax.axis_size("lon") * lax.axis_size("ens") * fields.shape[0]
     kcols = -(-cols // 128) * 128
-    n_chunks = len(chunks_of(cols)[0])
+    n_chunks = max(len(chunks_of(cols, width)[0]) for width in WIDTHS)
     anywhere = pl.BlockSpec(memory_space=pl.ANY)
     dma = pltpu.SemaphoreType.DMA
     out, grad, wgrad = pl.pallas_call(
@@ -647,23 +650,22 @@
             pltpu.VMEM((wcols, C), F32),
             pltpu.VMEM((C, wcols), F32),
             pltpu.VMEM((C // 2, wcols), F32),
-            pltpu.VMEM((C // 4, wcols), F32),
             pltpu.VMEM((lat_n - 1, share, wcols), F32),
-            pltpu.VMEM((share, wcols), F32),
+            pltpu.VMEM((2, share, wcols), F32),
             dma,
             dma((4,)),
             dma((2, n_chunks)),
             dma((2, 2)),
-            dma((2, 2, 2, n_chunks)),
-            dma((2, PANEL, n_chunks)),
+            dma((2, 2, 2, n_chunks, 2)),
+            dma((2, PANEL, n_chunks, 2)),
             dma((2, 3, 2, 2)),
             dma((2, PANEL, 2)),
-            dma((2,)),
-            dma((2,)),
-            dma((lat_n // 4,)),
+            dma((1,)),
+            dma((1,)),
+            dma((lat_n // 2,)),
             dma,
             dma((3,)),
-            dma,
+            dma((2,)),
         ],
         compiler_params=pltpu.CompilerParams(
             collective_id=0, has_side_effects=True, vmem_limit_bytes=61 * 1024 * 1024

time: 59.4 us -> 55.8 us (0.939)
  the two profiles are of different devices: /device:TPU:10 before, /device:TPU:1 now
where the time goes in v4:
time: 55.8 us; the launch traced here: 55.6 us
  Pallas kernels  55 us (99%)
  between operations  0.64 us (1%)
    pallas_call x1, Pallas kernels, shards(): pl.pallas_call(functools.partial(body, lat_n, cols, 1.0 / math.sqrt(total...  52.7 us
    pallas_call x1, Pallas kernels, shards(): pl.pallas_call(functools.partial(store, pieces), out_shape=[jax.ShapeDtyp...  2.33 us

profile of v4, /device:TPU:1, one launch (start us, length us, event | category | flops | bytes accessed | tf_op | source)
XLA Modules:
  0.0 55.6 jit_solution(9466215002140024492)
XLA Ops:
  0.6 52.7 %disco.1 = (bf16[2,720,256]{2,1,0:T(8,128)(2,1)}, bf16[2,720,256]{2,1,0:T(8,128)(2,1)}, f32[9,8,32]{2,1,0:T(8,128)}) custom-call(bf16[2,720,256]{2,1,0:T(8,128)(2,1)} %bitcast.7, bf16[2,720,256]{2,1,0:T(8,128)(2,1)} %bitcast.8, bf16[9,32,256]{2,1,0:T(8,128)(2,1)} %bitcast.9, bf16[5,9,5,64]{3,2,1,0:T(8,128)(2,1)} %bitcast.10, s32[5,64]{1,0:T(8,128)} %bitcast.11, ...), custom_call_target="tpu_custom_call" | custom-call | tf_op jit(solution)/shard_map/disco/pallas_call | solution.py:620
  53.3 2.3 %store.1 = (bf16[2,720,256]{2,1,0:T(8,128)(2,1)}, bf16[2,720,256]{2,1,0:T(8,128)(2,1)}, f32[9,8,32]{2,1,0:T(8,128)}) custom-call(bf16[2,720,256]{2,1,0:T(8,128)(2,1)} %get-tuple-element.9.refs_0_, bf16[2,720,256]{2,1,0:T(8,128)(2,1)} %get-tuple-element.10.refs_1_, f32[9,8,32]{2,1,0:T(8,128)} %get-tuple-element.11.refs_2_), custom_call_target="tpu_custom_call" | custom-call | tf_op jit(solution)/shard_map/store/pallas_call | solution.py:683

commit v5 on v4

--- a/solution.py
+++ b/solution.py
@@ -22,6 +22,7 @@
 NB = C // LW
 PB = LW // GW
 PANEL = 6
+HALO = (0, 1, 4, 5)
 WIDTHS = (256, 304)
 EARLY = 3
 PACE = (1, 1, 1)
@@ -33,7 +34,7 @@
     if len(starts) > 1 and cols - starts[-1] < 32:
         starts.pop()
     compute = [(s, (starts[j + 1] if j + 1 < len(starts) else cols) - s) for j, s in enumerate(starts)]
-    cuts = [0] + [s + 16 for s in starts[1:]] + [cols]
+    cuts = [0] + [s + PAD for s in starts[1:]] + [cols - PAD]
     send = [(cuts[j], cuts[j + 1] - cuts[j]) for j in range(len(starts))]
     pieces = []
     for start, size in send:
@@ -88,6 +89,8 @@
     row_recv,
     edge_send,
     edge_recv,
+    last_send,
+    last_recv,
     sum_send,
     sum_recv,
     share_send,
@@ -113,13 +116,11 @@
 
     @pl.when(jnp.logical_not(top))
     def _():
-        for to in (lon, sib):
-            pl.semaphore_signal(barrier, inc=1, device_id=(lat - 1, to, ens), device_id_type=MESH)
+        pl.semaphore_signal(barrier, inc=1, device_id=(lat - 1, lon, ens), device_id_type=MESH)
 
     @pl.when(jnp.logical_not(bottom))
     def _():
-        for to in (lon, sib):
-            pl.semaphore_signal(barrier, inc=1, device_id=(lat + 1, to, ens), device_id_type=MESH)
+        pl.semaphore_signal(barrier, inc=1, device_id=(lat + 1, lon, ens), device_id_type=MESH)
 
     n_shares = lat_n // 2
     share = C // lat_n
@@ -144,11 +145,11 @@
 
     pl.semaphore_wait(
         barrier,
-        7
+        5
         + n_shares
         - jnp.where(owner, 1, 0)
-        - 2 * jnp.where(top, 1, 0)
-        - 2 * jnp.where(bottom, 1, 0),
+        - jnp.where(top, 1, 0)
+        - jnp.where(bottom, 1, 0),
     )
 
     def own_copy(t, a):
@@ -181,57 +182,40 @@
             device_id_type=MESH,
         )
 
-    def edge_refs(t, a, slot, side):
-        src = sources[t].at[a, pl.ds(cols - PAD if side == 0 else 0, PAD)]
-        dst = panels[t].at[slot, pl.ds(0 if side == 0 else PAD + cols, PAD)]
-        return src, dst
-
-    def edge_copy(t, where_to, a, slot, side, to_lat, to_lon):
-        src, dst = edge_refs(t, a, slot, side)
+    def edge_copy(t, slot, side):
+        cells = pl.ds(cols - PAD if side == 0 else 0, PAD)
+        if slot in (2, 3):
+            src = sources[t].at[slot - 2, cells]
+        else:
+            src = panels[t].at[slot, pl.ds(cols if side == 0 else PAD, PAD)]
         return pltpu.make_async_remote_copy(
             src_ref=src,
-            dst_ref=dst,
-            send_sem=edge_send.at[t, where_to, a, side],
+            dst_ref=panels[t].at[slot, pl.ds(0 if side == 0 else PAD + cols, PAD)],
+            send_sem=edge_send.at[t, slot, side],
             recv_sem=edge_recv.at[t, slot, side],
+            device_id=(lat, sib, ens),
+            device_id_type=MESH,
+        )
+
+    def wait_edge(t, slot, side):
+        edge_copy(t, slot, side).wait_recv()
+
+    def last_copy(t, dirn, a):
+        to_lat, to_lon, slot = target(dirn, a)
+        return pltpu.make_async_remote_copy(
+            src_ref=sources[t].at[a, pl.ds(cols - PAD, PAD)],
+            dst_ref=panels[t].at[slot, pl.ds(cols, PAD)],
+            send_sem=last_send.at[t, dirn, a],
+            recv_sem=last_recv.at[t, slot],
             device_id=(to_lat, to_lon, ens),
             device_id_type=MESH,
         )
 
-    def edges(t):
-        for a in range(2):
-            for side in range(2):
-                edge_copy(t, 2, a, 2 + a, side, lat, sib).start()
-        for dirn, pole in ((0, top), (1, bottom)):
-            for a in range(2):
-                to_lat, _, slot = target(dirn, a)
-                for side in range(2):
-
-                    @pl.when(pole)
-                    def _():
-                        src, dst = edge_refs(t, a, slot, side)
-                        pltpu.make_async_copy(src, dst, edge_recv.at[t, slot, side]).start()
-
-                    @pl.when(jnp.logical_not(pole))
-                    def _():
-                        edge_copy(t, dirn, a, slot, side, to_lat, sib).start()
-
-    def edges_sent(t):
-        for a in range(2):
-            for side in range(2):
-                edge_copy(t, 2, a, 2 + a, side, lat, sib).wait_send()
-        for dirn, pole in ((0, top), (1, bottom)):
-            for a in range(2):
-                to_lat, _, slot = target(dirn, a)
-                for side in range(2):
-
-                    @pl.when(jnp.logical_not(pole))
-                    def _():
-                        edge_copy(t, dirn, a, slot, side, to_lat, sib).wait_send()
-
-    def wait_edge(t, slot):
-        for side in range(2):
-            src, dst = edge_refs(t, 0, slot, side)
-            pltpu.make_async_copy(dst, dst, edge_recv.at[t, slot, side]).wait()
+    def forward_last(t):
+        for slot in HALO:
+            dst = panels[t].at[slot, pl.ds(cols, PAD)]
+            pltpu.make_async_copy(dst, dst, last_recv.at[t, slot]).wait()
+            edge_copy(t, slot, 0).start()
 
     def wait_row(t, slot, ch):
         for h in range(2):
@@ -246,7 +230,11 @@
 
     orders = [[(ch, h) for ch in range(len(send)) for h in range(2)] for send in sends]
     for t in range(2):
-        edges(t)
+        for a in range(2):
+            for side in range(2):
+                edge_copy(t, 2 + a, side).start()
+            for dirn in range(2):
+                last_copy(t, dirn, a).start()
         for ch, h in orders[0] if t == 0 else orders[1][:EARLY]:
             send_rows(t, ch, h)
     small = [
@@ -348,7 +336,8 @@
     for t in range(2):
         for a in range(2):
             own_copy(t, a).wait()
-            wait_edge(t, 2 + a)
+            for side in range(2):
+                wait_edge(t, 2 + a, side)
             widen(t, 2 + a, 0, cols + 2 * PAD)
 
     def own_windows(b, carry):
@@ -396,12 +385,19 @@
     def arrive(t, ch):
         send = sends[t]
         start, size = send[ch][0][0], send[ch][0][1] + send[ch][1][1]
-        for slot in (0, 1, 4, 5):
+        if ch == 0:
+            forward_last(t)
+        for slot in HALO:
+            wait_row(t, slot, ch)
             if ch == 0:
-                wait_edge(t, slot)
-            wait_row(t, slot, ch)
+                edge_copy(t, slot, 1).start()
+        for slot in HALO:
+            if ch == 0:
+                wait_edge(t, slot, 0)
+            if ch == len(send) - 1:
+                wait_edge(t, slot, 1)
             lo = 0 if ch == 0 else PAD + start
-            hi = PAD + start + size + (PAD if ch == len(send) - 1 else 0)
+            hi = PAD + start + size + (2 * PAD if ch == len(send) - 1 else 0)
             widen(t, slot, lo, hi - lo)
 
     def transpose_rows(slots, start, end):
@@ -577,7 +573,12 @@
     for t in range(2):
         for ch in range(len(computes[t])):
             out_copy(t, ch).wait()
-        edges_sent(t)
+        for slot in range(PANEL):
+            for side in range(2):
+                edge_copy(t, slot, side).wait_send()
+        for a in range(2):
+            for dirn in range(2):
+                last_copy(t, dirn, a).wait_send()
         for ch in range(len(sends[t])):
             for dirn in range(2):
                 for a in range(2):
@@ -658,8 +659,10 @@
             dma((2, 2)),
             dma((2, 2, 2, n_chunks, 2)),
             dma((2, PANEL, n_chunks, 2)),
-            dma((2, 3, 2, 2)),
             dma((2, PANEL, 2)),
+            dma((2, PANEL, 2)),
+            dma((2, 2, 2)),
+            dma((2, PANEL)),
             dma((1,)),
             dma((1,)),
             dma((lat_n // 2,)),

time: 55.8 us -> 54.8 us (0.982)
  Pallas kernels: 55 us -> 54 us
    pallas_call x1, Pallas kernels: 52.7 us -> 51.6 us  [shards(): pl.pallas_call(functools.partial(body, lat_n, cols, 1.0 / math.sqrt(total...]
where the time goes in v5:
time: 54.8 us; the launch traced here: 54.6 us
  Pallas kernels  54 us (99%)
  between operations  0.64 us (1%)
    pallas_call x1, Pallas kernels, shards(): pl.pallas_call(functools.partial(body, lat_n, cols, 1.0 / math.sqrt(total...  51.6 us
    pallas_call x1, Pallas kernels, shards(): pl.pallas_call(functools.partial(store, pieces), out_shape=[jax.ShapeDtyp...  2.33 us

profile of v5, /device:TPU:1, one launch (start us, length us, event | category | flops | bytes accessed | tf_op | source)
XLA Modules:
  0.0 54.6 jit_solution(5489210897479089317)
XLA Ops:
  0.6 51.6 %disco.1 = (bf16[2,720,256]{2,1,0:T(8,128)(2,1)}, bf16[2,720,256]{2,1,0:T(8,128)(2,1)}, f32[9,8,32]{2,1,0:T(8,128)}) custom-call(bf16[2,720,256]{2,1,0:T(8,128)(2,1)} %bitcast.7, bf16[2,720,256]{2,1,0:T(8,128)(2,1)} %bitcast.8, bf16[9,32,256]{2,1,0:T(8,128)(2,1)} %bitcast.9, bf16[5,9,5,64]{3,2,1,0:T(8,128)(2,1)} %bitcast.10, s32[5,64]{1,0:T(8,128)} %bitcast.11, ...), custom_call_target="tpu_custom_call" | custom-call | tf_op jit(solution)/shard_map/disco/pallas_call | solution.py:621
  52.3 2.3 %store.1 = (bf16[2,720,256]{2,1,0:T(8,128)(2,1)}, bf16[2,720,256]{2,1,0:T(8,128)(2,1)}, f32[9,8,32]{2,1,0:T(8,128)}) custom-call(bf16[2,720,256]{2,1,0:T(8,128)(2,1)} %get-tuple-element.9.refs_0_, bf16[2,720,256]{2,1,0:T(8,128)(2,1)} %get-tuple-element.10.refs_1_, f32[9,8,32]{2,1,0:T(8,128)} %get-tuple-element.11.refs_2_), custom_call_target="tpu_custom_call" | custom-call | tf_op jit(solution)/shard_map/store/pallas_call | solution.py:686

commit v6 on v5

--- a/solution.py
+++ b/solution.py
@@ -23,7 +23,7 @@
 PB = LW // GW
 PANEL = 6
 HALO = (0, 1, 4, 5)
-WIDTHS = (256, 304)
+WIDTHS = (256, 288)
 EARLY = 3
 PACE = (1, 1, 1)
 TAPS = PANEL * WIN * LW
@@ -510,7 +510,7 @@
             low = pl.multiple_of(lon * half_rows, 8)
             wt[pl.ds(low, half_rows), :] += half[...]
             for j in range(n_shares):
-                to, copy = share_copy(j)
+                to, copy = share_copy(lax.rem(j + lat // 2, n_shares))
 
                 @pl.when(to != lat)
                 def _():
@@ -543,9 +543,9 @@
                 wout[k] = total[:, k * GW : (k + 1) * GW]
 
     sum_step(0)
+    sum_step(1)
     send_later(PACE[0])
     convolve(0, last, kf, out, 1)
-    sum_step(1)
     send_later(PACE[1])
     last = len(computes[1]) - 1
     for ch in range(last + 1):

time: 54.8 us -> 55 us (level)
  no operation moved by 1% of the time
where the time goes in v6:
time: 55 us; the launch traced here: 54.8 us
  Pallas kernels  54.1 us (98%)
  between operations  0.64 us (1%)
    pallas_call x1, Pallas kernels, shards(): pl.pallas_call(functools.partial(body, lat_n, cols, 1.0 / math.sqrt(total...  51.8 us
    pallas_call x1, Pallas kernels, shards(): pl.pallas_call(functools.partial(store, pieces), out_shape=[jax.ShapeDtyp...  2.33 us

profile of v6, /device:TPU:1, one launch (start us, length us, event | category | flops | bytes accessed | tf_op | source)
XLA Modules:
  0.0 54.8 jit_solution(5696477958945580247)
XLA Ops:
  0.6 51.8 %disco.1 = (bf16[2,720,256]{2,1,0:T(8,128)(2,1)}, bf16[2,720,256]{2,1,0:T(8,128)(2,1)}, f32[9,8,32]{2,1,0:T(8,128)}) custom-call(bf16[2,720,256]{2,1,0:T(8,128)(2,1)} %bitcast.7, bf16[2,720,256]{2,1,0:T(8,128)(2,1)} %bitcast.8, bf16[9,32,256]{2,1,0:T(8,128)(2,1)} %bitcast.9, bf16[5,9,5,64]{3,2,1,0:T(8,128)(2,1)} %bitcast.10, s32[5,64]{1,0:T(8,128)} %bitcast.11, ...), custom_call_target="tpu_custom_call" | custom-call | tf_op jit(solution)/shard_map/disco/pallas_call | solution.py:621
  52.5 2.3 %store.1 = (bf16[2,720,256]{2,1,0:T(8,128)(2,1)}, bf16[2,720,256]{2,1,0:T(8,128)(2,1)}, f32[9,8,32]{2,1,0:T(8,128)}) custom-call(bf16[2,720,256]{2,1,0:T(8,128)(2,1)} %get-tuple-element.9.refs_0_, bf16[2,720,256]{2,1,0:T(8,128)(2,1)} %get-tuple-element.10.refs_1_, f32[9,8,32]{2,1,0:T(8,128)} %get-tuple-element.11.refs_2_), custom_call_target="tpu_custom_call" | custom-call | tf_op jit(solution)/shard_map/store/pallas_call | solution.py:686

commit v7 on v5

--- a/solution.py
+++ b/solution.py
@@ -543,9 +543,9 @@
                 wout[k] = total[:, k * GW : (k + 1) * GW]
 
     sum_step(0)
+    sum_step(1)
     send_later(PACE[0])
     convolve(0, last, kf, out, 1)
-    sum_step(1)
     send_later(PACE[1])
     last = len(computes[1]) - 1
     for ch in range(last + 1):

time: 54.8 us -> 54.9 us (level)
  no operation moved by 1% of the time
where the time goes in v7:
time: 54.9 us; the launch traced here: 54.7 us
  Pallas kernels  54.1 us (99%)
  between operations  0.64 us (1%)
    pallas_call x1, Pallas kernels, shards(): pl.pallas_call(functools.partial(body, lat_n, cols, 1.0 / math.sqrt(total...  51.8 us
    pallas_call x1, Pallas kernels, shards(): pl.pallas_call(functools.partial(store, pieces), out_shape=[jax.ShapeDtyp...  2.33 us

profile of v7, /device:TPU:1, one launch (start us, length us, event | category | flops | bytes accessed | tf_op | source)
XLA Modules:
  0.0 54.7 jit_solution(14203686631518102248)
XLA Ops:
  0.6 51.8 %disco.1 = (bf16[2,720,256]{2,1,0:T(8,128)(2,1)}, bf16[2,720,256]{2,1,0:T(8,128)(2,1)}, f32[9,8,32]{2,1,0:T(8,128)}) custom-call(bf16[2,720,256]{2,1,0:T(8,128)(2,1)} %bitcast.7, bf16[2,720,256]{2,1,0:T(8,128)(2,1)} %bitcast.8, bf16[9,32,256]{2,1,0:T(8,128)(2,1)} %bitcast.9, bf16[5,9,5,64]{3,2,1,0:T(8,128)(2,1)} %bitcast.10, s32[5,64]{1,0:T(8,128)} %bitcast.11, ...), custom_call_target="tpu_custom_call" | custom-call | tf_op jit(solution)/shard_map/disco/pallas_call | solution.py:621
  52.4 2.3 %store.1 = (bf16[2,720,256]{2,1,0:T(8,128)(2,1)}, bf16[2,720,256]{2,1,0:T(8,128)(2,1)}, f32[9,8,32]{2,1,0:T(8,128)}) custom-call(bf16[2,720,256]{2,1,0:T(8,128)(2,1)} %get-tuple-element.9.refs_0_, bf16[2,720,256]{2,1,0:T(8,128)(2,1)} %get-tuple-element.10.refs_1_, f32[9,8,32]{2,1,0:T(8,128)} %get-tuple-element.11.refs_2_), custom_call_target="tpu_custom_call" | custom-call | tf_op jit(solution)/shard_map/store/pallas_call | solution.py:686
